TPU v7x, 256 devices: a whole 4x4x8 slice. The times are simulated.
256 devices in a mesh: pair: 2 (over z_hi), tensor: 4 (over x), dp: 32 (over y, z_lo, core).
Axes of the slice: x: 4, y: 4, z: 8 (z_hi: 2, z_lo: 4; z = z_hi * 4 + z_lo), core: 2. Of those that a mesh axis runs over, the one named last changes fastest.
Arguments:
- hidden_in: bfloat16 [32, 2, 384, 2560], P('dp', 'pair', 'tensor'), may hold values from -6 to 6
- queries: bfloat16 [32, 2, 384, 4096], P('dp', 'pair', None, 'tensor'), may hold values from -6 to 6
- key_states: bfloat16 [32, 2, 384, 512], P('dp', 'pair', None, 'tensor'), may hold values from -6 to 6
- value_states: bfloat16 [32, 2, 384, 512], P('dp', 'pair', None, 'tensor'), may hold values from -6 to 6
- out_weight: bfloat16 [4096, 2560], P('tensor', ('pair', 'dp')), may hold values from -0.09375 to 0.09375
- norm_gain: float32 [2560], replicated, may hold values from 0.25 to 1.75
- reward_head: float32 [2560], replicated, may hold values from -0.118585412 to 0.118585412
- lengths: int32 [32, 2], P('dp'), may hold values from 96 to 384, as said below
- labels: int32 [32], P('dp'), may hold values from 0 to 1
Outputs:
- layer_out: bfloat16 [32, 2, 384, 2560], P('dp', 'pair', 'tensor')
- pair_loss: float32 [32], P('dp')
- grad_queries: bfloat16 [32, 2, 384, 4096], P('dp', 'pair', None, 'tensor')
- grad_keys: bfloat16 [32, 2, 384, 512], P('dp', 'pair', None, 'tensor')
- grad_values: bfloat16 [32, 2, 384, 512], P('dp', 'pair', None, 'tensor')
- grad_out_weight: float32 [4096, 2560], P('tensor', ('pair', 'dp'))
Inputs may be any that keep to these rules, and one draw needn't show every extreme that they name: `lengths`: every response has at least 96 valid tokens; some response fills all 384 in every draw.
All inputs are finite; a program needn't handle non-finite values.
Results may differ from a plain program's by a relative error of at most 0.022.
Values may be sent and summed in bfloat16 or wider, within the bound.
A program may use at most 128 MiB of HBM per device.

v0:
```python
import jax
import jax.numpy as jnp
from jax import lax
from jax.sharding import PartitionSpec as P

HEAD_DIM = 128


loss_scale = 1024.0
norm_eps = 1e-06


def partner(value, axis, apart):
    mask = 2**apart
    pairs = [(source, source ^ mask) for source in range(lax.axis_size(axis))]
    return lax.ppermute(value, axis, pairs)


def visible(len_own, len_par, tok_all):
    row_ids = jnp.arange(tok_all, dtype=jnp.int32)[:, None]
    col_ids = jnp.arange(tok_all, dtype=jnp.int32)[None, :]
    own_seen = (col_ids <= row_ids) & (col_ids < len_own)
    par_seen = jnp.broadcast_to(col_ids < len_par, (tok_all, tok_all))
    return jnp.concatenate([own_seen, par_seen], axis=1)


def probability(query_rows, key_all, allowed):
    scores = jnp.einsum(
        "tkgd,skd->kgts", query_rows, key_all, preferred_element_type=jnp.float32
    ) * HEAD_DIM ** (-0.5)
    scores = jnp.where(allowed, scores, -1e30)
    row_max = jnp.max(scores, axis=-1, keepdims=True)
    exponent = jnp.where(allowed, jnp.exp(scores - row_max), 0.0)
    return exponent / jnp.sum(exponent, axis=-1, keepdims=True)


def per_device(
    hidden_in,
    queries,
    key_states,
    value_states,
    out_weight,
    norm_gain,
    reward_head,
    lengths,
    labels,
):
    tok_all = queries.shape[2]
    head_cols = queries.shape[3]
    kv_cols = key_states.shape[3]
    kv_local = kv_cols // HEAD_DIM
    groups = head_cols // HEAD_DIM // kv_local
    pair_side = lax.axis_index("pair")
    len_own = lengths[0, pair_side]
    len_par = lengths[0, 1 - pair_side]
    own_kv = jnp.stack([key_states[0, 0], value_states[0, 0]])
    far_kv = partner(own_kv, "pair", 0)
    key_all = jnp.concatenate([own_kv[0], far_kv[0]], axis=0).reshape(
        2 * tok_all, kv_local, HEAD_DIM
    )
    value_all = jnp.concatenate([own_kv[1], far_kv[1]], axis=0).reshape(
        2 * tok_all, kv_local, HEAD_DIM
    )
    allowed = visible(len_own, len_par, tok_all)
    query_rows = queries[0, 0].reshape(tok_all, kv_local, groups, HEAD_DIM)
    probs = probability(query_rows, key_all, allowed)
    weights = probs.astype(jnp.bfloat16)
    attended = jnp.einsum("kgts,skd->tkgd", weights, value_all, preferred_element_type=jnp.float32)
    attended = attended.reshape(tok_all, head_cols).astype(jnp.bfloat16)
    weights_full = lax.all_gather(out_weight, ("pair", "dp"), axis=1, tiled=True)
    row_count = hidden_in.shape[2]
    summed = lax.psum_scatter(
        jnp.dot(attended, weights_full, preferred_element_type=jnp.float32),
        "tensor",
        scatter_dimension=0,
        tiled=True,
    )
    layer_rows = (hidden_in[0, 0].astype(jnp.float32) + summed).astype(jnp.bfloat16)
    layer_f32 = layer_rows.astype(jnp.float32)
    inv_rms = lax.rsqrt(jnp.mean(layer_f32 * layer_f32, axis=-1, keepdims=True) + norm_eps)
    token_score = jnp.sum(layer_f32 * inv_rms * norm_gain * reward_head, axis=-1)
    positions = lax.axis_index("tensor") * row_count + jnp.arange(row_count, dtype=jnp.int32)
    valid_rows = (positions < len_own).astype(jnp.float32)
    len_root = jnp.sqrt(len_own.astype(jnp.float32))
    partial_reward = jnp.sum(token_score * valid_rows) / len_root
    placed = jnp.where(jnp.arange(2) == pair_side, partial_reward, 0.0)
    reward = lax.psum(placed, ("pair", "tensor"))
    label_sign = 2.0 * labels[0].astype(jnp.float32) - 1.0
    margin = label_sign * (reward[0] - reward[1])
    pair_loss = jnp.logaddexp(jnp.float32(0.0), -margin)
    first_slope = -label_sign * jax.nn.sigmoid(-margin) * loss_scale
    my_slope = jnp.where(pair_side == 0, first_slope, -first_slope)
    token_coef = (my_slope * valid_rows / len_root)[:, None]
    pull = token_coef * (norm_gain * reward_head)
    width_model = layer_f32.shape[1]
    grad_rows = (
        inv_rms * pull
        - layer_f32 * inv_rms**3 * jnp.sum(layer_f32 * pull, axis=-1, keepdims=True) / width_model
    ).astype(jnp.bfloat16)
    grad_full = lax.all_gather(grad_rows, "tensor", axis=0, tiled=True)
    grad_att = lax.dot_general(
        grad_full, weights_full, (((1,), (1,)), ((), ())), preferred_element_type=jnp.float32
    ).astype(jnp.bfloat16)
    weight_term = lax.dot_general(
        attended, grad_full, (((0,), (0,)), ((), ())), preferred_element_type=jnp.float32
    )
    grad_out_weight = lax.psum_scatter(weight_term, ("pair", "dp"), scatter_dimension=1, tiled=True)
    grad_here = grad_att.reshape(tok_all, kv_local, groups, HEAD_DIM)
    dprob = jnp.einsum("tkgd,skd->kgts", grad_here, value_all, preferred_element_type=jnp.float32)
    row_dot = jnp.sum(probs * dprob, axis=-1, keepdims=True)
    grad_scores = (probs * (dprob - row_dot) * HEAD_DIM ** (-0.5)).astype(jnp.bfloat16)
    grad_query = jnp.einsum(
        "kgts,skd->tkgd", grad_scores, key_all, preferred_element_type=jnp.float32
    )
    grad_query = grad_query.reshape(tok_all, head_cols).astype(jnp.bfloat16)
    key_terms = jnp.einsum(
        "kgts,tkgd->skd", grad_scores, query_rows, preferred_element_type=jnp.float32
    ).reshape(2 * tok_all, kv_cols)
    value_terms = jnp.einsum(
        "kgts,tkgd->skd", weights, grad_here, preferred_element_type=jnp.float32
    ).reshape(2 * tok_all, kv_cols)
    outgoing = jnp.stack([key_terms[tok_all:], value_terms[tok_all:]])
    incoming = partner(outgoing.astype(jnp.bfloat16), "pair", 0).astype(outgoing.dtype)
    grad_keys = (key_terms[:tok_all] + incoming[0]).astype(jnp.bfloat16)
    grad_values = (value_terms[:tok_all] + incoming[1]).astype(jnp.bfloat16)
    return (
        layer_rows[None, None],
        pair_loss[None],
        grad_query[None, None],
        grad_keys[None, None],
        grad_values[None, None],
        grad_out_weight,
    )


def solution(mesh):
    in_specs = (
        P("dp", "pair", "tensor", None),
        P("dp", "pair", None, "tensor"),
        P("dp", "pair", None, "tensor"),
        P("dp", "pair", None, "tensor"),
        P("tensor", ("pair", "dp")),
        P(),
        P(),
        P("dp", None),
        P("dp"),
    )
    out_specs = (
        P("dp", "pair", "tensor", None),
        P("dp"),
        P("dp", "pair", None, "tensor"),
        P("dp", "pair", None, "tensor"),
        P("dp", "pair", None, "tensor"),
        P("tensor", ("pair", "dp")),
    )
    return jax.shard_map(
        per_device, mesh=mesh, in_specs=in_specs, out_specs=out_specs, check_vma=False
    )
```

profile of v0, /device:TPU:1, one launch (start us, length us, event | category | flops | bytes accessed | tf_op | source)
XLA Modules:
  0.0 538.2 jit_solution(6959370064363291621)
XLA Ops:
  7.2 0.0 all-gather.3.cloned.1.call-start
  7.2 0.7 all-gather.3.cloned.1.call-update
  7.9 0.0 reduce-scatter.3.cloned.1.call-start
  7.9 1.0 pad_maximum_fusion
  8.9 7.8 %collective-permute-start = (bf16[2,384,128]{2,1,0:T(8,128)(2,1)S(1)}, bf16[2,384,128]{2,1,0:T(8,128)(2,1)S(1)}, u32[]{:S(2)}, u32[]{:S(2)}) collective-permute-start(bf16[2,384,128]{2,1,0:T(8,128)(2,1)S(1)} %pad_maximum_fusion), channel_id=1, source_target_pairs={{0,128},{128,0},{1,129},{129,1},{2,130},{130,2},{3,131},{131,3},{4... | collective-permute-start | bytes 589832 | tf_op jit(solution)/shard_map/ppermute | solution.py:16
  16.7 1.3 copy.38
  18.0 1.3 constant_dynamic-slice_fusion
  19.4 0.6 iota_compare_fusion.1
  20.0 0.7 iota_compare_fusion.2
  20.7 0.1 fusion.24
  20.8 0.2 pad_add_fusion
  21.1 2.6 fusion.4
  23.7 2.2 fusion.6
  25.9 2.5 convert_bitcast_fusion
  28.5 2.2 copy-done.1
  30.7 0.8 convolution_convert_fusion.1
  31.5 100.4 %all-gather.3.cloned.1.call-done = bf16[1024,2560]{0,1:T(8,128)(2,1)} async-done(((bf16[1024,40]{0,1:T(8,128)(2,1)}), bf16[1024,2560]{0,1:T(8,128)(2,1)}) %all-gather.3.cloned.1.call-update) | async-done | bytes 5242896 | tf_op jit(solution)/shard_map/all_gather | solution.py:70
  132.0 6.6 %fusion.39 = f32[384,2560]{1,0:T(8,128)} fusion(bf16[384,1024]{0,1:T(8,128)(2,1)S(1)} %bitcast.145, bf16[1024,2560]{0,1:T(8,128)(2,1)} %all-gather.3.cloned.1.call-done), kind=kOutput, calls=%fused_computation.78 | convolution fusion | flops 2013265920 | bytes 9961472 | tf_op jit(solution)/shard_map/dot_general | solution.py:73
  138.6 0.0 reduce-scatter.3.cloned.1.call-update
  138.6 0.0 all-gather.5.cloned.1.call-start
  140.0 43.6 %reduce-scatter.3.cloned.1.call-done = f32[96,2560]{1,0:T(8,128)} async-done(((f32[384,2560]{1,0:T(8,128)}), f32[96,2560]{1,0:T(8,128)}) %reduce-scatter.3.cloned.1.call-update) | async-done | bytes 983056 | tf_op jit(solution)/shard_map/reduce_scatter | solution.py:72
  183.6 1.4 fusion.10
  185.1 0.0 copy-start.3
  185.1 0.3 fusion.13
  185.4 1.2 fusion.31
  187.4 26.0 %psum.7 = f32[2]{0:T(128)S(1)} all-reduce(f32[2]{0:T(128)S(1)} %compare_select_fusion), channel_id=1, replica_groups=mesh['pair'=2,'tensor'=4,'dp'=32] {'pair','tensor'}, use_global_device_ids=true, to_apply=%region_6.7 | all-reduce | flops 2 | bytes 16 | tf_op jit(solution)/shard_map/psum | solution.py:87
  213.4 0.6 fusion.38
  215.4 0.7 fusion.32
  216.0 0.3 fusion.16
  216.3 1.3 fusion.9
  217.7 0.0 all-gather.5.cloned.1.call-update
  217.7 0.2 reduce-scatter.5.cloned.1.call-start
  217.9 30.2 %all-gather.5.cloned.1.call-done = bf16[384,2560]{1,0:T(8,128)(2,1)} async-done(((bf16[96,2560]{1,0:T(8,128)(2,1)}), bf16[384,2560]{1,0:T(8,128)(2,1)}) %all-gather.5.cloned.1.call-update) | async-done | bytes 1966096 | tf_op jit(solution)/shard_map/all_gather | solution.py:100
  248.1 7.0 %fusion.40 = f32[1024,2560]{0,1:T(8,128)} fusion(bf16[384,1024]{0,1:T(8,128)(2,1)S(1)} %bitcast.146, bf16[384,2560]{1,0:T(8,128)(2,1)} %all-gather.5.cloned.1.call-done), kind=kOutput, calls=%fused_computation.79 | convolution fusion | flops 2013265920 | bytes 13238272 | tf_op jit(solution)/shard_map/dot_general | solution.py:104
  255.2 0.0 reduce-scatter.5.cloned.1.call-update
  255.2 7.2 %copy.31 = bf16[8,384,768]{2,0,1:T(8,128)(2,1)} copy(bf16[8,384,768]{1,2,0:T(8,128)(2,1)} %copy-done.1) | data formatting | bytes 9437184 | tf_op jit(solution)/shard_map/reshape.6
  262.6 5.4 %convolution_convert_fusion.2 = bf16[384,1024]{1,0:T(8,128)(2,1)S(1)} fusion(bf16[384,2560]{1,0:T(8,128)(2,1)} %all-gather.5.cloned.1.call-done, bf16[1024,2560]{0,1:T(8,128)(2,1)} %all-gather.3.cloned.1.call-done), kind=kOutput, calls=%fused_computation.20 | convolution fusion | flops 2013659136 | bytes 7995392 | tf_op jit(solution)/shard_map/dot_general | solution.py:101
  268.0 0.2 copy.39
  268.2 1.9 convolution_bitcast_fusion
  270.2 3.6 fusion
  273.8 3.9 fusion.7
  277.7 1.4 convolution_bitcast_fusion.1
  279.2 5.5 %collective-permute-start.1 = (bf16[2,384,128]{2,1,0:T(8,128)(2,1)S(1)}, bf16[2,384,128]{2,1,0:T(8,128)(2,1)S(1)}, u32[]{:S(2)}, u32[]{:S(2)}) collective-permute-start(bf16[2,384,128]{2,1,0:T(8,128)(2,1)S(1)} %pad_maximum_fusion.1), channel_id=1, source_target_pairs={{0,128},{128,0},{1,129},{129,1},{2,130},{130,2},{3,131},{131,3},{4... | collective-permute-start | bytes 589832 | tf_op jit(solution)/shard_map/ppermute | solution.py:16
  284.7 0.8 convolution_convert_fusion
  285.5 1.2 copy.25
  286.7 7.0 %collective-permute-done.1 = bf16[2,384,128]{2,1,0:T(8,128)(2,1)S(1)} collective-permute-done((bf16[2,384,128]{2,1,0:T(8,128)(2,1)S(1)}, bf16[2,384,128]{2,1,0:T(8,128)(2,1)S(1)}, u32[]{:S(2)}, u32[]{:S(2)}) %collective-permute-start.1) | collective-permute-done | bytes 196640 | tf_op jit(solution)/shard_map/ppermute | solution.py:16
  293.7 1.6 fusion.26
  295.4 235.2 %reduce-scatter.5.cloned.1.call-done = f32[1024,40]{0,1:T(8,128)} async-done(((f32[1024,2560]{0,1:T(8,128)}), f32[1024,40]{0,1:T(8,128)}) %reduce-scatter.5.cloned.1.call-update) | async-done | bytes 163856 | tf_op jit(solution)/shard_map/reduce_scatter | solution.py:107
  (40 shorter events, 0.2 us)
Async XLA Ops:
  7.2 124.8 %all-gather.3.cloned.1.call-start = ((), (), s32[]{:S(2)}) async-start(), calls=%async_computation.2 | async-start | bytes 5324800 | tf_op jit(solution)/shard_map/all_gather | solution.py:70
  7.9 175.7 %reduce-scatter.3.cloned.1.call-start = ((), (), s32[]{:S(2)}) async-start(), calls=%async_computation.3 | async-start | bytes 4915200 | tf_op jit(solution)/shard_map/reduce_scatter | solution.py:72
  8.9 12.1 %collective-permute-start = (bf16[2,384,128]{2,1,0:T(8,128)(2,1)S(1)}, bf16[2,384,128]{2,1,0:T(8,128)(2,1)S(1)}, u32[]{:S(2)}, u32[]{:S(2)}) collective-permute-start(bf16[2,384,128]{2,1,0:T(8,128)(2,1)S(1)} %pad_maximum_fusion), channel_id=1, source_target_pairs={{0,128},{128,0},{1,129},{129,1},{2,130},{130,2},{3,131},{131,3},{4... | collective-permute-start | bytes 589832 | tf_op jit(solution)/shard_map/ppermute | solution.py:16
  21.1 7.4 %copy-start.9 = (bf16[384,128]{1,0:T(8,128)(2,1)}, bf16[384,128]{1,0:T(8,128)(2,1)S(1)}, u32[]{:S(2)}) copy-start(bf16[384,128]{1,0:T(8,128)(2,1)S(1)} %get-tuple-element.16) | copy-start | bytes 294916
  23.6 4.8 copy-start
  25.9 4.7 copy-start.7
  28.5 2.2 copy-start.1
  31.5 108.5 %copy-start.11 = (f32[2560]{0:T(1024)S(1)}, f32[2560]{0:T(1024)}, u32[]{:S(2)}) copy-start(f32[2560]{0:T(1024)} %param.15) | copy-start | bytes 30724
  31.5 108.5 %copy-start.12 = (f32[2560]{0:T(1024)S(1)}, f32[2560]{0:T(1024)}, u32[]{:S(2)}) copy-start(f32[2560]{0:T(1024)} %param.14) | copy-start | bytes 30724
  31.5 152.1 %copy-start.6 = (bf16[1,1,96,2560]{3,2,1,0:T(8,128)(2,1)S(1)}, bf16[1,1,96,2560]{3,2,1,0:T(8,128)(2,1)}, u32[]{:S(2)}) copy-start(bf16[1,1,96,2560]{3,2,1,0:T(8,128)(2,1)} %param.9) | copy-start | bytes 1474564
  138.6 109.6 %all-gather.5.cloned.1.call-start = ((), (), s32[]{:S(2)}) async-start(), calls=%async_computation.4 | async-start | bytes 2457600 | tf_op jit(solution)/shard_map/all_gather | solution.py:100
  185.1 70.1 %copy-start.3 = (bf16[96,2560]{1,0:T(8,128)(2,1)}, bf16[96,2560]{1,0:T(8,128)(2,1)S(1)}, u32[]{:S(2)}) copy-start(bf16[96,2560]{1,0:T(8,128)(2,1)S(1)} %get-tuple-element.13) | copy-start | bytes 1474564
  217.7 312.9 %reduce-scatter.5.cloned.1.call-start = ((), (), s32[]{:S(2)}) async-start(), calls=%async_computation.5 | async-start | bytes 10649600 | tf_op jit(solution)/shard_map/reduce_scatter | solution.py:107
  255.2 15.0 %slice-start = ((s8[9437184]{0:T(1024)(128)(4,1)}), s8[1048576]{0:T(1024)(128)(4,1)S(1)}, s32[]{:S(2)}) async-start(s8[9437184]{0:T(1024)(128)(4,1)} %bitcast.142), calls=%async_computation.6 | async-start | bytes 2097152
  262.6 5.7 %copy-start.2 = (bf16[8,384,768]{2,0,1:T(8,128)(2,1)S(1)}, bf16[8,384,768]{2,0,1:T(8,128)(2,1)}, u32[]{:S(2)}) copy-start(bf16[8,384,768]{2,0,1:T(8,128)(2,1)} %copy.31) | copy-start | bytes 14155780
  262.6 7.6 %slice-start.1 = ((s8[9437184]{0:T(1024)(128)(4,1)}), s8[4194304]{0:T(1024)(128)(4,1)S(1)}, s32[]{:S(2)}) async-start(s8[9437184]{0:T(1024)(128)(4,1)} %bitcast.142), calls=%async_computation.7 | async-start | bytes 8388608
  262.6 7.6 %slice-start.2 = ((s8[9437184]{0:T(1024)(128)(4,1)}), s8[4194304]{0:T(1024)(128)(4,1)S(1)}, s32[]{:S(2)}) async-start(s8[9437184]{0:T(1024)(128)(4,1)} %bitcast.142), calls=%async_computation.8 | async-start | bytes 8388608
  262.6 7.6 %copy-start.8 = (bf16[1,1,384,128]{3,2,1,0:T(8,128)(2,1)S(1)}, bf16[1,1,384,128]{3,2,1,0:T(8,128)(2,1)}, u32[]{:S(2)}) copy-start(bf16[1,1,384,128]{3,2,1,0:T(8,128)(2,1)} %param.12) | copy-start | bytes 294916
  262.6 7.6 %copy-start.10 = (bf16[384,128]{1,0:T(8,128)(2,1)S(1)}, bf16[384,128]{1,0:T(8,128)(2,1)}, u32[]{:S(2)}) copy-start(bf16[384,128]{1,0:T(8,128)(2,1)} %copy-done.9) | copy-start | bytes 294916
  270.2 8.9 %copy-start.4 = (f32[768,1,128]{2,0,1:T(8,128)}, f32[768,1,128]{2,0,1:T(8,128)S(1)}, u32[]{:S(2)}) copy-start(f32[768,1,128]{2,0,1:T(8,128)S(1)} %convolution_bitcast_fusion) | copy-start | bytes 1179652
  273.8 10.9 %copy-start.5 = (bf16[1,1,384,128]{3,2,1,0:T(8,128)(2,1)S(1)}, bf16[1,1,384,128]{3,2,1,0:T(8,128)(2,1)}, u32[]{:S(2)}) copy-start(bf16[1,1,384,128]{3,2,1,0:T(8,128)(2,1)} %param.11) | copy-start | bytes 294916
  279.2 14.5 %collective-permute-start.1 = (bf16[2,384,128]{2,1,0:T(8,128)(2,1)S(1)}, bf16[2,384,128]{2,1,0:T(8,128)(2,1)S(1)}, u32[]{:S(2)}, u32[]{:S(2)}) collective-permute-start(bf16[2,384,128]{2,1,0:T(8,128)(2,1)S(1)} %pad_maximum_fusion.1), channel_id=1, source_target_pairs={{0,128},{128,0},{1,129},{129,1},{2,130},{130,2},{3,131},{131,3},{4... | collective-permute-start | bytes 589832 | tf_op jit(solution)/shard_map/ppermute | solution.py:16
Sparse Core Ops, SparseCore 0:
  9.9 122.0 all-gather.2
  138.7 44.8 reduce-scatter.2
  217.8 30.2 all-gather.4
  255.3 275.1 reduce-scatter.4
where the time goes:
time: 543 us; the launch traced here: 538 us
  waiting for transfers between devices  417 us (77%)
  matrix products  30.1 us (6%)
  blocking collectives  26 us (5%)
  between operations  18.8 us (3%)
  other arithmetic  18.2 us (3%)
  local copies, waits for them, and re-layouts  14.1 us (3%)
  starting transfers between devices  13.7 us (3%)
    reduce_scatter x1, waiting for transfers between devices, per_device(): lax.psum_scatter(weight_term, ('pair', 'dp'), scatter_dimension=1, tiled=...  235 us
    all_gather x1, waiting for transfers between devices, per_device(): lax.all_gather(out_weight, ('pair', 'dp'), axis=1, tiled=True)  100 us
    reduce_scatter x1, waiting for transfers between devices, per_device(): lax.psum_scatter(jnp.dot(attended, weights_full, preferred_element_type=j...  43.6 us
    all_gather x1, waiting for transfers between devices, per_device(): grad_full = lax.all_gather(grad_rows, 'tensor', axis=0, tiled=True)  30.2 us
    psum x1, blocking collectives, per_device(): reward = lax.psum(placed, ('pair', 'tensor'))  26 us
    ppermute x2, starting transfers between devices, partner(): return lax.ppermute(value, axis, pairs)  13.4 us
  transfers between devices with their start and end apart: 6, of which 5 were waited for; matrix products, arithmetic and copies ran while one was open for 8% of the time, Pallas kernels for 0%

commit v1 on v0

v1 whole, which is shorter than its diff:
```python
from types import SimpleNamespace

import jax
import jax.numpy as jnp
from jax import lax
from jax.experimental import pallas as pl
from jax.experimental.pallas import tpu as pltpu
from jax.sharding import PartitionSpec as P

HEAD_DIM = 128
LOSS_SCALE = 1024.0
NORM_EPS = 1e-06
LOG2E = 1.4426950408889634

TOK = 384
WIDTH = 2560
HEADS = 8
NX, NY, NZ = 4, 4, 8
ROWS = TOK // NX
CHUNKS = 4
CW = WIDTH // CHUNKS
BLK = 80
HALF = 512
LA = 384
LB = HALF - LA

MESH = pl.DeviceIdType.MESH
F32 = jnp.float32
BF16 = jnp.bfloat16

NT = (((1,), (1,)), ((), ()))
TN = (((0,), (0,)), ((), ()))
NN = (((1,), (0,)), ((), ()))


def mm(a, b, dims):
    return lax.dot_general(a, b, dims, preferred_element_type=F32)


def device(x, y, z, c):
    return (z // 4, x, y * 8 + lax.rem(z, 4) * 2 + c)


def rcopy(src, dst, send, recv, dev):
    return pltpu.make_async_remote_copy(
        src_ref=src, dst_ref=dst, send_sem=send, recv_sem=recv, device_id=dev, device_id_type=MESH
    )


DMA = pltpu.SemaphoreType.DMA
ARGS = (
    "lens",
    "labels",
    "hidden",
    "q",
    "k",
    "v",
    "wt",
    "gain",
    "head",
    "layer_o",
    "loss_o",
    "dq_o",
    "dk_o",
    "dv_o",
    "gw_o",
)
SCRATCH = dict(
    wh=pltpu.VMEM((2, 2, NY, 4, BLK, HALF), BF16),
    wf=pltpu.VMEM((2, 40, HALF), F32),
    qv=pltpu.VMEM((TOK, HEADS * HEAD_DIM), BF16),
    hv=pltpu.VMEM((ROWS, WIDTH), BF16),
    lv=pltpu.VMEM((ROWS, WIDTH), BF16),
    dqv=pltpu.VMEM((TOK, HEADS * HEAD_DIM), BF16),
    asm=pltpu.VMEM((BLK, HALF), F32),
    kall=pltpu.VMEM((2 * TOK, HEAD_DIM), BF16),
    vall=pltpu.VMEM((2 * TOK, HEAD_DIM), BF16),
    ktr=pltpu.VMEM((HEAD_DIM, 2 * TOK), BF16),
    vtr=pltpu.VMEM((HEAD_DIM, 2 * TOK), BF16),
    bias=pltpu.VMEM((2 * TOK, TOK), F32),
    lse=pltpu.VMEM((HEADS, 1, TOK), F32),
    att=pltpu.VMEM((2, TOK, HALF), BF16),
    acc=pltpu.VMEM((CHUNKS, NX, ROWS, CW), F32),
    xs=pltpu.VMEM((CHUNKS, NX, ROWS, CW), BF16),
    xr=pltpu.VMEM((3, CHUNKS, ROWS, CW), BF16),
    gf=pltpu.VMEM((CHUNKS, NX, ROWS, CW), BF16),
    rw=pltpu.VMEM((2, NX, 8, 128), F32),
    own=pltpu.VMEM((CHUNKS, CW, HALF), F32),
    mo=pltpu.VMEM((CHUNKS, CW, HALF), BF16),
    mi=pltpu.VMEM((CHUNKS, CW, HALF), BF16),
    red=pltpu.VMEM((2, NY, 4, BLK, HALF), BF16),
    yl=pltpu.VMEM((3, 2, 4, BLK, LA), BF16),
    zsend=pltpu.VMEM((2, 4, BLK, LA), BF16),
    zl=pltpu.VMEM((7, BLK, LA), BF16),
    z2l=pltpu.VMEM((7, 2, 2, BLK, LB), BF16),
    y2send=pltpu.VMEM((NY, BLK, LB), BF16),
    y2l=pltpu.VMEM((3, BLK, LB), BF16),
    gwc=pltpu.VMEM((BLK, HALF), F32),
    gwr=pltpu.VMEM((40, HALF), F32),
    gacc=pltpu.VMEM((2, TOK, HALF), F32),
    gatt=pltpu.VMEM((2, TOK, HALF), BF16),
    dk=pltpu.VMEM((2 * TOK, HEAD_DIM), F32),
    dv=pltpu.VMEM((2 * TOK, HEAD_DIM), F32),
    dkv_out=pltpu.VMEM((2, TOK, HEAD_DIM), BF16),
    dkv_in=pltpu.VMEM((2, TOK, HEAD_DIM), BF16),
    s_kv=DMA((4,)),
    r_kv=DMA((4,)),
    s_c=DMA((4,)),
    r_c=DMA((4,)),
    s_z=DMA((7,)),
    r_z=DMA((7,)),
    s_y=DMA((3, 8)),
    r_y=DMA((3, 8)),
    s_z2=DMA((7,)),
    r_z2=DMA((7,)),
    s_x=DMA((3, CHUNKS)),
    r_x=DMA((3, CHUNKS)),
    s_g=DMA((3, CHUNKS)),
    r_g=DMA((3, CHUNKS)),
    s_rw=DMA((7,)),
    r_rw=DMA((7,)),
    s_m=DMA((CHUNKS,)),
    r_m=DMA((CHUNKS,)),
    t_z=DMA((7,)),
    u_z=DMA((7,)),
    t_y=DMA((3, 2)),
    u_y=DMA((3, 2)),
    t_z2=DMA((7, 2)),
    u_z2=DMA((7, 2)),
    loc=DMA((8,)),
    out_l=DMA((CHUNKS,)),
    out_q=DMA((HEADS,)),
    t_y2=DMA((3,)),
    u_y2=DMA((3,)),
)


def kernel(*refs):
    names = SimpleNamespace(**dict(zip(ARGS + tuple(SCRATCH), refs)))
    run(names)


def run(n):
    lens = n.lens
    labels = n.labels
    hidden = n.hidden
    q = n.q
    k = n.k
    v = n.v
    wt = n.wt
    gain = n.gain
    head = n.head
    layer_o = n.layer_o
    loss_o = n.loss_o
    dq_o = n.dq_o
    dk_o = n.dk_o
    dv_o = n.dv_o
    gw_o = n.gw_o
    wh = n.wh
    wf = n.wf
    qv = n.qv
    hv = n.hv
    lv = n.lv
    dqv = n.dqv
    asm = n.asm
    kall = n.kall
    vall = n.vall
    ktr = n.ktr
    vtr = n.vtr
    bias = n.bias
    lse = n.lse
    att = n.att
    acc = n.acc
    xs = n.xs
    xr = n.xr
    gf = n.gf
    rw = n.rw
    own = n.own
    mo = n.mo
    mi = n.mi
    red = n.red
    yl = n.yl
    zsend = n.zsend
    zl = n.zl
    z2l = n.z2l
    y2send = n.y2send
    y2l = n.y2l
    gwc = n.gwc
    gwr = n.gwr
    gacc = n.gacc
    gatt = n.gatt
    dk = n.dk
    dv = n.dv
    dkv_out = n.dkv_out
    dkv_in = n.dkv_in
    s_kv = n.s_kv
    r_kv = n.r_kv
    s_c = n.s_c
    r_c = n.r_c
    s_z = n.s_z
    r_z = n.r_z
    s_y = n.s_y
    r_y = n.r_y
    s_z2 = n.s_z2
    r_z2 = n.r_z2
    s_x = n.s_x
    r_x = n.r_x
    s_g = n.s_g
    r_g = n.r_g
    s_rw = n.s_rw
    r_rw = n.r_rw
    s_m = n.s_m
    r_m = n.r_m
    t_z = n.t_z
    u_z = n.u_z
    t_y = n.t_y
    u_y = n.u_y
    t_z2 = n.t_z2
    u_z2 = n.u_z2
    loc = n.loc
    out_l = n.out_l
    out_q = n.out_q
    t_y2 = n.t_y2
    u_y2 = n.u_y2

    pair = lax.axis_index("pair")
    x = lax.axis_index("tensor")
    dp = lax.axis_index("dp")
    y = dp // 8
    zlo = lax.rem(dp // 2, 4)
    z = pair * 4 + zlo
    c = lax.rem(dp, 2)
    mate = 1 - c

    def xdev(d):
        return device(lax.rem(x + d, NX), y, z, c)

    def ydev(d):
        return device(x, lax.rem(y + d, NY), z, c)

    def zdev(d):
        return device(x, y, lax.rem(z + d, NZ), c)

    core = device(x, y, z, mate)
    far = zdev(4)

    def rwdev(i):
        dpair, dx = i // 4, i % 4
        return device(lax.rem(x + dx, NX), y, lax.rem(z + 4 * dpair, NZ), c)

    local = [
        pltpu.make_async_copy(k, kall.at[pl.ds(0, TOK)], loc.at[0]),
        pltpu.make_async_copy(v, vall.at[pl.ds(0, TOK)], loc.at[1]),
        pltpu.make_async_copy(q, qv, loc.at[2]),
    ]
    load_hidden = pltpu.make_async_copy(hidden, hv, loc.at[3])
    for cp in local + [load_hidden]:
        cp.start()

    barrier = pltpu.get_barrier_semaphore()
    peers = [core]
    peers += [rwdev(i) for i in range(1, 8)]
    peers += [ydev(d) for d in (1, 2, 3)]
    peers += [zdev(d) for d in (1, 2, 3, 5, 6, 7)]
    for peer in peers:
        pl.semaphore_signal(barrier, inc=1, device_id=peer, device_id_type=MESH)

    len_own = jnp.where(pair == 0, lens[0, 0], lens[0, 1])
    len_par = jnp.where(pair == 0, lens[0, 1], lens[0, 0])
    key_id = lax.broadcasted_iota(jnp.int32, (TOK, TOK), 0)
    tok_id = lax.broadcasted_iota(jnp.int32, (TOK, TOK), 1)
    bias[0:TOK, :] = jnp.where((key_id <= tok_id) & (key_id < len_own), 0.0, -1e30)
    bias[TOK:, :] = jnp.where(key_id < len_par, 0.0, -1e30)

    for half in range(2):
        wf[half] = wt[:, pl.ds(half * HALF, HALF)].astype(F32)

    pl.semaphore_wait(barrier, len(peers))

    kv_copies = [
        rcopy(k, kall.at[pl.ds(TOK, TOK)], s_kv.at[0], r_kv.at[0], far),
        rcopy(v, vall.at[pl.ds(TOK, TOK)], s_kv.at[1], r_kv.at[1], far),
    ]
    mine = pl.ds(pl.multiple_of(c * 40, 8), 40)
    wcore = rcopy(wf.at[mate], asm.at[mine], s_c.at[0], r_c.at[0], core)
    wcore.start()
    for cp in kv_copies:
        cp.start()

    asm[mine, :] = wf[c]
    wcore.wait()
    wh[c, pair, y, zlo] = asm[...].astype(BF16)

    own_all = wh.at[c, pair, y, zlo]
    own_a = wh.at[c, pair, y, zlo, :, pl.ds(0, LA)]
    y0 = [rcopy(own_all, own_all, s_y.at[d - 1, 0], r_y.at[d - 1, 0], ydev(d)) for d in range(1, NY)]

    def hop(e):
        there = lax.rem(pair + e // 4, 2) * 4 + lax.rem(zlo + e, 4)
        return there, lax.rem(there - z + NZ, NZ)

    def za_copy(d):
        return rcopy(own_a, own_a, s_z.at[d - 1], r_z.at[d - 1], zdev(d))

    for cp in y0:
        cp.start()
    for e in range(1, 8):
        za_copy(hop(e)[1]).start()

    for cp in y0:
        cp.wait()
    part_b = wh.at[c, pair, :, zlo, :, pl.ds(LA, LB)]

    def zb_copy(d):
        return rcopy(part_b, part_b, s_z2.at[d - 1], r_z2.at[d - 1], zdev(d))

    for e in range(1, 8):
        zb_copy(hop(e)[1]).start()

    for cp in local + kv_copies:
        cp.wait()
    ktr[...] = jnp.transpose(kall[...].astype(F32)).astype(BF16)
    vtr[...] = jnp.transpose(vall[...].astype(F32)).astype(BF16)

    def ya_copy(e, d):
        there, _ = hop(e)
        part = wh.at[c, there // 4, y, lax.rem(there, 4), :, pl.ds(0, LA)]
        return rcopy(part, part, s_y.at[d - 1, e], r_y.at[d - 1, e], ydev(d))

    scale2 = HEAD_DIM ** (-0.5) * LOG2E

    def forward(h, carry):
        cols = pl.ds(pl.multiple_of(h * HEAD_DIM, HEAD_DIM), HEAD_DIM)
        s = mm(kall[...], qv[:, cols], NT) * scale2 + bias[...]
        top = jnp.max(s, axis=0, keepdims=True)
        e = jnp.exp2(s - top)
        total = jnp.sum(e, axis=0, keepdims=True)
        out = mm(vtr[...], e.astype(BF16), NN) * (1.0 / total)
        lane = pl.ds(pl.multiple_of(lax.rem(h, 4) * HEAD_DIM, HEAD_DIM), HEAD_DIM)
        att[h // 4, :, lane] = jnp.transpose(out).astype(BF16)
        lse[h] = top + jnp.log2(total)
        return carry

    def forward_relay(h, carry):
        forward(h, carry)
        e = h + 1
        _, there = hop(e)
        za_copy(NZ - there).wait_recv()
        for d in (2, 1, 3):
            ya_copy(e, d).start()
        return carry

    lax.fori_loop(0, HEADS - 1, forward_relay, 0)
    forward(HEADS - 1, 0)

    def wrows(half, j):
        return wh[half, j // 2, pl.ds(lax.rem(j, 2) * 2, 2)].reshape(CW, HALF)

    def project_own(i, carry):
        j = lax.rem(i + 2 * pair, CHUNKS)
        acc[j] = mm(att[c], wrows(c, j), NT).reshape(NX, ROWS, CW)
        return carry

    def xcopy(d, j):
        return rcopy(
            xs.at[j, lax.rem(x + d, NX)], xr.at[d - 1, j], s_x.at[d - 1, j], r_x.at[d - 1, j], xdev(d)
        )

    def project_rest(i, carry):
        j = lax.rem(i + 2 * pair, CHUNKS)
        p = acc[j] + mm(att[mate], wrows(mate, j), NT).reshape(NX, ROWS, CW)
        acc[j] = p
        xs[j] = p.astype(BF16)
        for d in (2, 1, 3):
            xcopy(d, j).start()
        return carry

    for part in range(2):
        for e in range(4 * part, 4 * part + 4):
            if e > 0:
                zb_copy(NZ - hop(e)[1]).wait_recv()
                for d in (1, 2, 3):
                    ya_copy(e, d).wait_recv()
        zh = lax.rem(pair + part, 2)
        swap = rcopy(wh.at[c, zh], wh.at[c, zh], s_c.at[1 + part], r_c.at[1 + part], core)
        swap.start()
        lax.fori_loop(2 * part, 2 * part + 2, project_own, 0)
        swap.wait()
        lax.fori_loop(2 * part, 2 * part + 2, project_rest, 0)
    for e in range(1, 8):
        za_copy(e).wait_send()
        zb_copy(e).wait_send()
        for d in (1, 2, 3):
            ya_copy(e, d).wait_send()
    load_hidden.wait()

    def layer_copy(j):
        cols = pl.ds(pl.multiple_of(j * CW, 128), CW)
        return pltpu.make_async_copy(lv.at[:, cols], layer_o.at[:, cols], out_l.at[j])

    def layer(i, carry):
        square, along = carry
        j = lax.rem(i + 2 * pair, CHUNKS)
        for d in (1, 2, 3):
            xcopy(d, j).wait()
        cols = pl.ds(pl.multiple_of(j * CW, 128), CW)
        total = hv[:, cols].astype(F32) + acc[j, x]
        for d in (1, 2, 3):
            total += xr[d - 1, j].astype(F32)
        rounded = total.astype(BF16)
        lv[:, cols] = rounded
        layer_copy(j).start()
        value = rounded.astype(F32)
        factor = gain[:, cols] * head[:, cols]
        square += jnp.sum(value * value, axis=1, keepdims=True)
        along += jnp.sum(value * factor, axis=1, keepdims=True)
        return square, along

    zero = jnp.zeros((ROWS, 1), F32)
    square, along = lax.fori_loop(0, CHUNKS, layer, (zero, zero))
    inv = lax.rsqrt(square * (1.0 / WIDTH) + NORM_EPS)
    position = x * ROWS + lax.broadcasted_iota(jnp.int32, (ROWS, 1), 0)
    valid = jnp.where(position < len_own, 1.0, 0.0)
    root = jnp.sqrt(jnp.full((ROWS, 1), len_own, jnp.int32).astype(F32))
    weight = valid / root
    partial = jnp.sum(inv * along * weight, axis=0, keepdims=True)
    rw[pair, x] = jnp.broadcast_to(partial, (8, 128))
    own_rw = rw.at[pair, x]
    rw_copies = [rcopy(own_rw, own_rw, s_rw.at[i - 1], r_rw.at[i - 1], rwdev(i)) for i in range(1, 8)]
    for cp in rw_copies:
        cp.start()

    gscale = inv * weight
    gcorr = inv * inv * inv * along * weight * (1.0 / WIDTH)

    def gcopy(d, j):
        own = gf.at[j, x]
        return rcopy(own, own, s_g.at[d - 1, j], r_g.at[d - 1, j], xdev(d))

    def rows_grad(i, carry):
        j = lax.rem(i + 2 * pair, CHUNKS)
        cols = pl.ds(pl.multiple_of(j * CW, 128), CW)
        factor = gain[:, cols] * head[:, cols]
        value = lv[:, cols].astype(F32)
        gf[j, x] = (gscale * factor - value * gcorr).astype(BF16)
        for d in (2, 1, 3):
            gcopy(d, j).start()
        return carry

    lax.fori_loop(0, CHUNKS, rows_grad, 0)

    for cp in rw_copies:
        cp.wait()
    reward0 = rw[0, 0] + rw[0, 1] + rw[0, 2] + rw[0, 3]
    reward1 = rw[1, 0] + rw[1, 1] + rw[1, 2] + rw[1, 3]
    sign = 2.0 * jnp.full((8, 128), labels[0], jnp.int32).astype(F32) - 1.0
    margin = sign * (reward0 - reward1)
    loss_o[...] = jnp.maximum(-margin, 0.0) + jnp.log1p(jnp.exp(-jnp.abs(margin)))
    first = -sign * jax.nn.sigmoid(-margin) * LOSS_SCALE
    side = jnp.where(pair == 0, 1.0, -1.0)
    slope = (first * side)[0:1, 0:1]

    def mcopy(j):
        return rcopy(mo.at[j], mi.at[j], s_m.at[j], r_m.at[j], core)

    gacc[...] = jnp.zeros_like(gacc)

    def products(i):
        j = lax.rem(i + 2 * pair, CHUNKS)
        for d in (1, 2, 3):
            gcopy(d, j).wait()
        g = gf[j].reshape(TOK, CW)
        mo[j] = (mm(g, att[mate], TN) * slope).astype(BF16)
        mcopy(j).start()
        own[j] = mm(g, att[c], TN) * slope
        for half in range(2):
            gacc[half] += mm(g, wrows(half, j), NN)

    def ycopy2(d, zh):
        src = red.at[zh, lax.rem(y + d, NY), :, :, pl.ds(0, LA)]
        return rcopy(src, yl.at[d - 1, zh], t_y.at[d - 1, zh], u_y.at[d - 1, zh], ydev(d))

    def zcopy2(d, yp):
        to = lax.rem(z + d, NZ)
        src = red.at[to // 4, pl.ds(2 * yp, 2), lax.rem(to, 4), :, pl.ds(LA, LB)]
        return rcopy(src, z2l.at[d - 1, yp], t_z2.at[d - 1, yp], u_z2.at[d - 1, yp], zdev(d))

    def merge(i):
        j = lax.rem(i + 2 * pair, CHUNKS)
        zh = j // 2
        yp = lax.rem(j, 2)
        mcopy(j).wait()
        both = own[j] + mi[j].astype(F32)
        red[zh, pl.ds(yp * 2, 2)] = both.astype(BF16).reshape(2, 4, BLK, HALF)
        for d in (2, 1, 3):
            @pl.when(lax.rem(y + d, NY) // 2 == yp)
            def _():
                ycopy2(d, zh).start()
        for d in (4, 3, 5, 2, 6, 1, 7):
            @pl.when(lax.rem(z + d, NZ) // 4 == zh)
            def _():
                zcopy2(d, yp).start()

    def step(i, carry):
        products(i)
        merge(i - 1)
        return carry

    products(0)
    lax.fori_loop(1, CHUNKS, step, 0)
    merge(CHUNKS - 1)

    gatt[...] = gacc[...].astype(BF16)
    dk[...] = jnp.zeros_like(dk)
    dv[...] = jnp.zeros_like(dv)
    slope_scaled = slope * HEAD_DIM ** (-0.5)

    def dq_copy(h):
        cols = pl.ds(pl.multiple_of(h * HEAD_DIM, HEAD_DIM), HEAD_DIM)
        return pltpu.make_async_copy(dqv.at[:, cols], dq_o.at[:, cols], out_q.at[h])

    def backward(h, carry):
        cols = pl.ds(pl.multiple_of(h * HEAD_DIM, HEAD_DIM), HEAD_DIM)
        lane = pl.ds(pl.multiple_of(lax.rem(h, 4) * HEAD_DIM, HEAD_DIM), HEAD_DIM)
        qh = qv[:, cols]
        gh = gatt[h // 4, :, lane]
        p = jnp.exp2(mm(kall[...], qh, NT) * scale2 + bias[...] - lse[h])
        dprob = mm(vall[...], gh, NT)
        delta = jnp.sum(p * dprob, axis=0, keepdims=True)
        ds = (p * (dprob - delta)).astype(BF16)
        dv[...] += mm(p.astype(BF16), gh, NN)
        dk[...] += mm(ds, qh, NN)
        dqv[:, cols] = (jnp.transpose(mm(ktr[...], ds, NN)) * slope_scaled).astype(BF16)
        dq_copy(h).start()
        return carry

    def zcopy1(d):
        to = lax.rem(z + d, NZ)
        src = zsend.at[to // 4, lax.rem(to, 4)]
        return rcopy(src, zl.at[d - 1], t_z.at[d - 1], u_z.at[d - 1], zdev(d))

    def ysum(part):
        zh = lax.rem(pair + part, 2)
        total = red[zh, y, :, :, pl.ds(0, LA)].astype(F32)
        for d in (1, 2, 3):
            ycopy2(d, zh).wait_recv()
            total += yl[d - 1, zh].astype(F32)
        zsend[zh] = total.astype(BF16)
        for e in range(4 * part, 4 * part + 4):
            if e > 0:
                zcopy1(hop(e)[1]).start()

    lax.fori_loop(0, 2, backward, 0)
    ysum(0)
    lax.fori_loop(2, 5, backward, 0)
    ysum(1)
    lax.fori_loop(5, HEADS, backward, 0)

    dkv_out[0] = (dk[TOK:, :] * slope_scaled).astype(BF16)
    dkv_out[1] = (dv[TOK:, :] * slope).astype(BF16)
    back = [rcopy(dkv_out.at[i], dkv_in.at[i], s_kv.at[2 + i], r_kv.at[2 + i], far) for i in range(2)]
    for cp in back:
        cp.start()

    part = red[pair, :, zlo, :, pl.ds(LA, LB)].astype(F32).reshape(2, 2, BLK, LB)
    for d in range(1, 8):
        for yp in range(2):
            zcopy2(d, yp).wait()
        part += z2l[d - 1].astype(F32)
    y2send[...] = part.astype(BF16).reshape(NY, BLK, LB)
    yb2 = []
    for d in (2, 1, 3):
        src = y2send.at[lax.rem(y + d, NY)]
        yb2.append(rcopy(src, y2l.at[d - 1], t_y2.at[d - 1], u_y2.at[d - 1], ydev(d)))
        yb2[-1].start()
    for d in range(1, 8):
        zcopy1(d).wait()
    for d in (1, 2, 3):
        for zh in range(2):
            ycopy2(d, zh).wait_send()
    part = zsend[pair, zlo].astype(F32)
    for d in range(7):
        part += zl[d].astype(F32)
    gwc[:, 0:LA] = part
    for cp in yb2:
        cp.wait()
    part = y2send[y].astype(F32)
    for d in range(3):
        part += y2l[d].astype(F32)
    gwc[:, LA:] = part
    mate_rows = gwc.at[pl.ds(pl.multiple_of(mate * 40, 8), 40)]
    gswap = rcopy(mate_rows, gwr, s_c.at[3], r_c.at[3], core)
    gswap.start()
    gw_o[:, pl.ds(pl.multiple_of(c * HALF, HALF), HALF)] = gwc[mine, :]
    gswap.wait()
    gw_o[:, pl.ds(pl.multiple_of(mate * HALF, HALF), HALF)] = gwr[...]

    for j in range(CHUNKS):
        layer_copy(j).wait()
    for h in range(HEADS):
        dq_copy(h).wait()
    for cp in back:
        cp.wait()
    dk_o[...] = (dk[0:TOK, :] * slope_scaled + dkv_in[0].astype(F32)).astype(BF16)
    dv_o[...] = (dv[0:TOK, :] * slope + dkv_in[1].astype(F32)).astype(BF16)


def per_device(hidden_in, queries, key_states, value_states, out_weight, norm_gain, reward_head, lengths, labels):
    smem = pl.BlockSpec(memory_space=pltpu.SMEM)
    vmem = pl.BlockSpec(memory_space=pltpu.VMEM)
    hbm = pl.BlockSpec(memory_space=pl.ANY)
    layer_rows, loss, grad_query, grad_keys, grad_values, grad_weight = pl.pallas_call(
        kernel,
        out_shape=(
            jax.ShapeDtypeStruct((ROWS, WIDTH), BF16),
            jax.ShapeDtypeStruct((8, 128), F32),
            jax.ShapeDtypeStruct((TOK, HEADS * HEAD_DIM), BF16),
            jax.ShapeDtypeStruct((TOK, HEAD_DIM), BF16),
            jax.ShapeDtypeStruct((TOK, HEAD_DIM), BF16),
            jax.ShapeDtypeStruct((40, 2 * HALF), F32),
        ),
        in_specs=[smem, smem] + [hbm] * 4 + [vmem] * 3,
        out_specs=(hbm, vmem, hbm, vmem, vmem, vmem),
        scratch_shapes=list(SCRATCH.values()),
        compiler_params=pltpu.CompilerParams(
            collective_id=0, has_side_effects=True, vmem_limit_bytes=60 * 2**20
        ),
        cost_estimate=pl.CostEstimate(flops=12 * 10**9, bytes_accessed=10 * 2**20, transcendentals=0),
    )(
        lengths,
        labels,
        hidden_in[0, 0],
        queries[0, 0],
        key_states[0, 0],
        value_states[0, 0],
        out_weight.T,
        norm_gain[None],
        reward_head[None],
    )
    return (
        layer_rows[None, None],
        loss[0, 0:1],
        grad_query[None, None],
        grad_keys[None, None],
        grad_values[None, None],
        grad_weight.T,
    )


def solution(mesh):
    in_specs = (
        P("dp", "pair", "tensor", None),
        P("dp", "pair", None, "tensor"),
        P("dp", "pair", None, "tensor"),
        P("dp", "pair", None, "tensor"),
        P("tensor", ("pair", "dp")),
        P(),
        P(),
        P("dp", None),
        P("dp"),
    )
    out_specs = (
        P("dp", "pair", "tensor", None),
        P("dp"),
        P("dp", "pair", None, "tensor"),
        P("dp", "pair", None, "tensor"),
        P("dp", "pair", None, "tensor"),
        P("tensor", ("pair", "dp")),
    )
    return jax.shard_map(
        per_device, mesh=mesh, in_specs=in_specs, out_specs=out_specs, check_vma=False
    )
```

time: 543 us -> 145 us (0.27)
  waiting for transfers between devices: 417 us -> 0 us
  Pallas kernels: 0 us -> 134 us
  matrix products: 30.1 us -> 0 us
  blocking collectives: 26 us -> 0 us
  other arithmetic: 18.2 us -> 0 us
  between operations: 18.8 us -> 1.31 us
  starting transfers between devices: 13.7 us -> 0 us
  local copies, waits for them, and re-layouts: 14.1 us -> 7.95 us
    reduce_scatter x2 -> x0, waiting for transfers between devices: 279 us -> none  [the longest x1 235 us: per_device(): lax.psum_scatter(weight_term, ('pair', 'dp'), scatter_dimension=1, tiled=...]
    pallas_call x0 -> x1, Pallas kernels: none -> 134 us  [per_device(): pl.pallas_call(kernel, out_shape=(jax.ShapeDtypeStruct((ROWS, WIDTH), BF1...]
    all_gather x2 -> x0, waiting for transfers between devices: 131 us -> none  [the longest x1 100 us: per_device(): lax.all_gather(out_weight, ('pair', 'dp'), axis=1, tiled=True)]
    dot_general x9 -> x0, matrix products: 30.1 us -> none  [the longest x1 7.05 us: per_device(): lax.dot_general(attended, grad_full, (((0,), (0,)), ((), ())), preferred_...]
    psum x1 -> x0, blocking collectives: 26 us -> none  [per_device(): reward = lax.psum(placed, ('pair', 'tensor'))]
    ppermute x2 -> x0, starting transfers between devices: 13.4 us -> none  [partner(): return lax.ppermute(value, axis, pairs)]
    another operation x4 -> x0, other arithmetic: 7.4 us -> none
    another operation x2 -> x0, local copies, waits for them, and re-layouts: 7.28 us -> none
  transfers between devices with their start and end apart: 6 -> 0, of which waited for: 5 -> 0; matrix products, arithmetic and copies ran while one was open for 8% -> 0% of each run, Pallas kernels for 0% -> 0%
where the time goes in v1:
time: 145 us; the launch traced here: 143 us
  Pallas kernels  134 us (92%)
  local copies, waits for them, and re-layouts  7.95 us (5%)
    pallas_call x1, Pallas kernels, per_device(): pl.pallas_call(kernel, out_shape=(jax.ShapeDtypeStruct((ROWS, WIDTH), BF1...  134 us
    unnamed x15, local copies, waits for them, and re-layouts  4.76 us

profile of v1, /device:TPU:1, one launch (start us, length us, event | category | flops | bytes accessed | tf_op | source)
XLA Modules:
  0.0 143.3 jit_solution(3366353027762959240)
XLA Ops:
  1.3 0.0 copy-start.4
  1.3 1.3 broadcast_in_dim.18.refs_7_
  2.6 0.0 copy-done.4
  2.6 0.6 broadcast_in_dim.19.refs_8_
  3.2 134.1 %shard_map.136 = (bf16[96,2560]{1,0:T(8,128)(2,1)}, f32[8,128]{1,0:T(8,128)}, bf16[384,1024]{1,0:T(8,128)(2,1)}, bf16[384,128]{1,0:T(8,128)(2,1)}, bf16[384,128]{1,0:T(8,128)(2,1)}, /*index=5*/f32[40,1024]{1,0:T(8,128)}) custom-call(s32[1,2]{1,0:T(1,128)} %refs_0_.1, s32[1]{0:T(128)S(6)} %copy.20.refs_1_, bf16[96,2560]{1,0:T(8,128)(2,1)} %bitcast.17, ...), custom_call_target="tpu_custom_call" | custom-call | flops 12000000000 | bytes 10485760 | tf_op jit(solution)/shard_map/pallas_call | solution.py:612
  137.3 0.0 copy-start
  137.3 1.3 slice.3
  138.6 1.8 %copy.21 = bf16[1,1,96,2560]{3,2,1,0:T(8,128)(2,1)} copy(bf16[1,1,96,2560]{3,2,1,0:T(8,128)(2,1)} %bitcast.12) | data formatting | bytes 983040
  140.4 0.0 copy-done
  140.4 0.0 copy-start.3
  140.4 0.0 copy-start.2
  140.4 0.9 copy.22
  141.3 0.1 copy-done.3
  141.4 0.0 copy-start.1
  141.4 0.6 copy.23
  142.0 0.0 copy-done.2
  142.0 0.6 copy.24
  142.7 0.0 copy-done.1
  142.7 0.7 copy.25
Async XLA Ops:
  1.3 1.3 copy-start.4
  137.3 3.1 %copy-start = (bf16[384,1024]{1,0:T(8,128)(2,1)S(1)}, bf16[384,1024]{1,0:T(8,128)(2,1)}, u32[]{:S(2)}) copy-start(bf16[384,1024]{1,0:T(8,128)(2,1)} %get-tuple-element.14) | copy-start | bytes 2359300
  140.4 1.0 copy-start.3
  140.4 1.6 %copy-start.2 = (bf16[384,128]{1,0:T(8,128)(2,1)S(1)}, bf16[384,128]{1,0:T(8,128)(2,1)}, u32[]{:S(2)}) copy-start(bf16[384,128]{1,0:T(8,128)(2,1)} %get-tuple-element.16) | copy-start | bytes 294916
  141.4 1.3 copy-start.1

commit v2 on v1

--- a/solution.py
+++ b/solution.py
@@ -21,6 +21,8 @@
 CW = WIDTH // CHUNKS
 BLK = 80
 HALF = 512
+HR = ROWS // 2
+HL = HALF // 2
 LA = 384
 LB = HALF - LA
 
@@ -78,23 +80,31 @@
     ktr=pltpu.VMEM((HEAD_DIM, 2 * TOK), BF16),
     vtr=pltpu.VMEM((HEAD_DIM, 2 * TOK), BF16),
     bias=pltpu.VMEM((2 * TOK, TOK), F32),
+    peak=pltpu.VMEM((HEADS, 1, TOK), F32),
+    mass=pltpu.VMEM((HEADS, 1, TOK), F32),
+    part_out=pltpu.VMEM((HEADS, HEAD_DIM, TOK), F32),
     lse=pltpu.VMEM((HEADS, 1, TOK), F32),
     att=pltpu.VMEM((2, TOK, HALF), BF16),
     acc=pltpu.VMEM((CHUNKS, NX, ROWS, CW), F32),
     xs=pltpu.VMEM((CHUNKS, NX, ROWS, CW), BF16),
-    xr=pltpu.VMEM((3, CHUNKS, ROWS, CW), BF16),
+    xin=pltpu.VMEM((2, CHUNKS, ROWS, CW), BF16),
+    xrel=pltpu.VMEM((2, CHUNKS, HR, CW), BF16),
+    xro=pltpu.VMEM((2, CHUNKS, HR, CW), BF16),
     gf=pltpu.VMEM((CHUNKS, NX, ROWS, CW), BF16),
     rw=pltpu.VMEM((2, NX, 8, 128), F32),
     own=pltpu.VMEM((CHUNKS, CW, HALF), F32),
     mo=pltpu.VMEM((CHUNKS, CW, HALF), BF16),
     mi=pltpu.VMEM((CHUNKS, CW, HALF), BF16),
     red=pltpu.VMEM((2, NY, 4, BLK, HALF), BF16),
-    yl=pltpu.VMEM((3, 2, 4, BLK, LA), BF16),
+    yin=pltpu.VMEM((2, 2, 4, BLK, LA), BF16),
+    yrel=pltpu.VMEM((2, 2, 2, BLK, LA), BF16),
+    yro=pltpu.VMEM((2, 2, 2, BLK, LA), BF16),
     zsend=pltpu.VMEM((2, 4, BLK, LA), BF16),
     zl=pltpu.VMEM((7, BLK, LA), BF16),
     z2l=pltpu.VMEM((7, 2, 2, BLK, LB), BF16),
     y2send=pltpu.VMEM((NY, BLK, LB), BF16),
     y2l=pltpu.VMEM((3, BLK, LB), BF16),
+    factor=pltpu.VMEM((1, WIDTH), F32),
     gwc=pltpu.VMEM((BLK, HALF), F32),
     gwr=pltpu.VMEM((40, HALF), F32),
     gacc=pltpu.VMEM((2, TOK, HALF), F32),
@@ -107,24 +117,24 @@
     r_kv=DMA((4,)),
     s_c=DMA((4,)),
     r_c=DMA((4,)),
-    s_z=DMA((7,)),
-    r_z=DMA((7,)),
-    s_y=DMA((3, 8)),
-    r_y=DMA((3, 8)),
-    s_z2=DMA((7,)),
-    r_z2=DMA((7,)),
-    s_x=DMA((3, CHUNKS)),
-    r_x=DMA((3, CHUNKS)),
-    s_g=DMA((3, CHUNKS)),
-    r_g=DMA((3, CHUNKS)),
-    s_rw=DMA((7,)),
-    r_rw=DMA((7,)),
+    s_z=DMA((8,)),
+    r_z=DMA((8,)),
+    s_w=DMA((8,)),
+    r_w=DMA((8,)),
+    s_y=DMA((4, 8)),
+    r_y=DMA((4, 8)),
+    s_x=DMA((3, 2, CHUNKS)),
+    r_x=DMA((3, 2, CHUNKS)),
+    s_g=DMA((2, 2, CHUNKS)),
+    r_g=DMA((2, 2, CHUNKS)),
+    s_rw=DMA((4,)),
+    r_rw=DMA((4,)),
     s_m=DMA((CHUNKS,)),
     r_m=DMA((CHUNKS,)),
     t_z=DMA((7,)),
     u_z=DMA((7,)),
-    t_y=DMA((3, 2)),
-    u_y=DMA((3, 2)),
+    t_y=DMA((3, 2, 2)),
+    u_y=DMA((3, 2, 2)),
     t_z2=DMA((7, 2)),
     u_z2=DMA((7, 2)),
     loc=DMA((8,)),
@@ -168,23 +178,31 @@
     ktr = n.ktr
     vtr = n.vtr
     bias = n.bias
+    peak = n.peak
+    mass = n.mass
+    part_out = n.part_out
     lse = n.lse
     att = n.att
     acc = n.acc
     xs = n.xs
-    xr = n.xr
+    xin = n.xin
+    xrel = n.xrel
+    xro = n.xro
     gf = n.gf
     rw = n.rw
     own = n.own
     mo = n.mo
     mi = n.mi
     red = n.red
-    yl = n.yl
+    yin = n.yin
+    yrel = n.yrel
+    yro = n.yro
     zsend = n.zsend
     zl = n.zl
     z2l = n.z2l
     y2send = n.y2send
     y2l = n.y2l
+    factor = n.factor
     gwc = n.gwc
     gwr = n.gwr
     gacc = n.gacc
@@ -199,10 +217,10 @@
     r_c = n.r_c
     s_z = n.s_z
     r_z = n.r_z
+    s_w = n.s_w
+    r_w = n.r_w
     s_y = n.s_y
     r_y = n.r_y
-    s_z2 = n.s_z2
-    r_z2 = n.r_z2
     s_x = n.s_x
     r_x = n.r_x
     s_g = n.s_g
@@ -244,10 +262,6 @@
     core = device(x, y, z, mate)
     far = zdev(4)
 
-    def rwdev(i):
-        dpair, dx = i // 4, i % 4
-        return device(lax.rem(x + dx, NX), y, lax.rem(z + 4 * dpair, NZ), c)
-
     local = [
         pltpu.make_async_copy(k, kall.at[pl.ds(0, TOK)], loc.at[0]),
         pltpu.make_async_copy(v, vall.at[pl.ds(0, TOK)], loc.at[1]),
@@ -259,9 +273,9 @@
 
     barrier = pltpu.get_barrier_semaphore()
     peers = [core]
-    peers += [rwdev(i) for i in range(1, 8)]
+    peers += [xdev(d) for d in (1, 2, 3)]
     peers += [ydev(d) for d in (1, 2, 3)]
-    peers += [zdev(d) for d in (1, 2, 3, 5, 6, 7)]
+    peers += [zdev(d) for d in range(1, NZ)]
     for peer in peers:
         pl.semaphore_signal(barrier, inc=1, device_id=peer, device_id_type=MESH)
 
@@ -274,6 +288,8 @@
 
     for half in range(2):
         wf[half] = wt[:, pl.ds(half * HALF, HALF)].astype(F32)
+
+    factor[...] = (gain[...] * head[...]).reshape(1, WIDTH)
 
     pl.semaphore_wait(barrier, len(peers))
 
@@ -284,74 +300,113 @@
     mine = pl.ds(pl.multiple_of(c * 40, 8), 40)
     wcore = rcopy(wf.at[mate], asm.at[mine], s_c.at[0], r_c.at[0], core)
     wcore.start()
-    for cp in kv_copies:
-        cp.start()
 
     asm[mine, :] = wf[c]
     wcore.wait()
     wh[c, pair, y, zlo] = asm[...].astype(BF16)
 
-    own_all = wh.at[c, pair, y, zlo]
-    own_a = wh.at[c, pair, y, zlo, :, pl.ds(0, LA)]
-    y0 = [rcopy(own_all, own_all, s_y.at[d - 1, 0], r_y.at[d - 1, 0], ydev(d)) for d in range(1, NY)]
+    steps = (0, 7, 1, 6, 2, 5, 3, 4)
 
     def hop(e):
         there = lax.rem(pair + e // 4, 2) * 4 + lax.rem(zlo + e, 4)
         return there, lax.rem(there - z + NZ, NZ)
 
-    def za_copy(d):
-        return rcopy(own_a, own_a, s_z.at[d - 1], r_z.at[d - 1], zdev(d))
-
-    for cp in y0:
-        cp.start()
-    for e in range(1, 8):
-        za_copy(hop(e)[1]).start()
-
-    for cp in y0:
+    def block(row, e):
+        there = lax.rem(z + steps[e], NZ)
+        return wh.at[c, there // 4, row, lax.rem(there, 4)]
+
+    def zcopy(e):
+        part = block(y, 0 if e <= 2 else e - 2)
+        return rcopy(part, part, s_z.at[e], r_z.at[e], zdev(1 if e % 2 else 7))
+
+    def ycopy(s, e):
+        part = block(y, e)
+        return rcopy(part, part, s_y.at[s, e], r_y.at[s, e], ydev(1 + 2 * s))
+
+    def ypass(s, e):
+        part = block(lax.rem(y + 3 - 2 * s, NY), e).at[:, pl.ds(s * HL, HL)]
+        return rcopy(part, part, s_y.at[2 + s, e], r_y.at[2 + s, e], ydev(1 + 2 * s))
+
+    def swap(e):
+        there = lax.rem(z + steps[e], NZ)
+        part = wh.at[c, there // 4, :, lax.rem(there, 4)]
+        return rcopy(part, part, s_w.at[e], r_w.at[e], core)
+
+    def yforward(e):
+        for s in range(2):
+            ycopy(s, e).wait_recv()
+        for s in range(2):
+            ypass(s, e).start()
+
+    def hand(e):
+        for s in range(2):
+            ypass(s, e).wait_recv()
+        swap(e).start()
+
+    def serve(e):
+        zcopy(e).wait_recv()
+        if e + 2 < 8:
+            zcopy(e + 2).start()
+        for s in range(2):
+            ycopy(s, e).start()
+        yforward(e - 1)
+        if e == 3:
+            for cp in kv_copies:
+                cp.start()
+        if e >= 3:
+            hand(e - 3)
+
+    for e in (1, 2):
+        zcopy(e).start()
+    for s in range(2):
+        ycopy(s, 0).start()
+
+    scale2 = HEAD_DIM ** (-0.5) * LOG2E
+    for cp in local:
         cp.wait()
-    part_b = wh.at[c, pair, :, zlo, :, pl.ds(LA, LB)]
-
-    def zb_copy(d):
-        return rcopy(part_b, part_b, s_z2.at[d - 1], r_z2.at[d - 1], zdev(d))
-
-    for e in range(1, 8):
-        zb_copy(hop(e)[1]).start()
-
-    for cp in local + kv_copies:
-        cp.wait()
-    ktr[...] = jnp.transpose(kall[...].astype(F32)).astype(BF16)
-    vtr[...] = jnp.transpose(vall[...].astype(F32)).astype(BF16)
-
-    def ya_copy(e, d):
-        there, _ = hop(e)
-        part = wh.at[c, there // 4, y, lax.rem(there, 4), :, pl.ds(0, LA)]
-        return rcopy(part, part, s_y.at[d - 1, e], r_y.at[d - 1, e], ydev(d))
-
-    scale2 = HEAD_DIM ** (-0.5) * LOG2E
-
-    def forward(h, carry):
+    ktr[:, 0:TOK] = jnp.transpose(kall[0:TOK, :].astype(F32)).astype(BF16)
+    vtr[:, 0:TOK] = jnp.transpose(vall[0:TOK, :].astype(F32)).astype(BF16)
+
+    def softmax_part(h, rows):
         cols = pl.ds(pl.multiple_of(h * HEAD_DIM, HEAD_DIM), HEAD_DIM)
-        s = mm(kall[...], qv[:, cols], NT) * scale2 + bias[...]
+        s = mm(kall[rows, :], qv[:, cols], NT) * scale2 + bias[rows, :]
         top = jnp.max(s, axis=0, keepdims=True)
         e = jnp.exp2(s - top)
         total = jnp.sum(e, axis=0, keepdims=True)
-        out = mm(vtr[...], e.astype(BF16), NN) * (1.0 / total)
+        return top, total, mm(vtr[:, rows], e.astype(BF16), NN)
+
+    def forward_own(h, carry):
+        peak[h], mass[h], part_out[h] = softmax_part(h, pl.ds(0, TOK))
+        return carry
+
+    def forward_far(h, carry):
+        top1, total1, out1 = peak[h], mass[h], part_out[h]
+        top2, total2, out2 = softmax_part(h, pl.ds(TOK, TOK))
+        top = jnp.maximum(top1, top2)
+        fac1, fac2 = jnp.exp2(top1 - top), jnp.exp2(top2 - top)
+        total = total1 * fac1 + total2 * fac2
+        out = out1 * (fac1 / total) + out2 * (fac2 / total)
         lane = pl.ds(pl.multiple_of(lax.rem(h, 4) * HEAD_DIM, HEAD_DIM), HEAD_DIM)
         att[h // 4, :, lane] = jnp.transpose(out).astype(BF16)
         lse[h] = top + jnp.log2(total)
         return carry
 
-    def forward_relay(h, carry):
-        forward(h, carry)
-        e = h + 1
-        _, there = hop(e)
-        za_copy(NZ - there).wait_recv()
-        for d in (2, 1, 3):
-            ya_copy(e, d).start()
-        return carry
-
-    lax.fori_loop(0, HEADS - 1, forward_relay, 0)
-    forward(HEADS - 1, 0)
+    for e in range(1, 7):
+        lax.fori_loop(e - 1, e, forward_own, 0)
+        serve(e)
+    lax.fori_loop(6, HEADS, forward_own, 0)
+    serve(7)
+    for cp in kv_copies:
+        cp.wait()
+    ktr[:, TOK:] = jnp.transpose(kall[TOK:, :].astype(F32)).astype(BF16)
+    vtr[:, TOK:] = jnp.transpose(vall[TOK:, :].astype(F32)).astype(BF16)
+    lax.fori_loop(0, 2, forward_far, 0)
+    yforward(7)
+    hand(5)
+    lax.fori_loop(2, 6, forward_far, 0)
+    hand(6)
+    hand(7)
+    lax.fori_loop(6, HEADS, forward_far, 0)
 
     def wrows(half, j):
         return wh[half, j // 2, pl.ds(lax.rem(j, 2) * 2, 2)].reshape(CW, HALF)
@@ -361,37 +416,67 @@
         acc[j] = mm(att[c], wrows(c, j), NT).reshape(NX, ROWS, CW)
         return carry
 
-    def xcopy(d, j):
-        return rcopy(
-            xs.at[j, lax.rem(x + d, NX)], xr.at[d - 1, j], s_x.at[d - 1, j], r_x.at[d - 1, j], xdev(d)
-        )
+    def xcopy(kind, t, j):
+        near = 1 + 2 * t
+        if kind == 0:
+            src, dst = xs.at[j, lax.rem(x + 2, NX), pl.ds(HR * t, HR)], xrel.at[t, j]
+        elif kind == 1:
+            rows = pl.ds(HR * (1 - t), HR)
+            src, dst = xs.at[j, lax.rem(x + near, NX), rows], xin.at[t, j, rows]
+        else:
+            src, dst = xro.at[t, j], xin.at[t, j, pl.ds(HR * t, HR)]
+        return rcopy(src, dst, s_x.at[kind, t, j], r_x.at[kind, t, j], xdev(near))
+
+    def xstart(i):
+        j = lax.rem(i + 2 * pair, CHUNKS)
+        for kind in range(2):
+            for t in range(2):
+                xcopy(kind, t, j).start()
+
+    def xsent(i):
+        j = lax.rem(i + 2 * pair, CHUNKS)
+        for kind in range(2):
+            for t in range(2):
+                xcopy(kind, t, j).wait_send()
 
     def project_rest(i, carry):
         j = lax.rem(i + 2 * pair, CHUNKS)
         p = acc[j] + mm(att[mate], wrows(mate, j), NT).reshape(NX, ROWS, CW)
         acc[j] = p
         xs[j] = p.astype(BF16)
-        for d in (2, 1, 3):
-            xcopy(d, j).start()
         return carry
 
-    for part in range(2):
-        for e in range(4 * part, 4 * part + 4):
-            if e > 0:
-                zb_copy(NZ - hop(e)[1]).wait_recv()
-                for d in (1, 2, 3):
-                    ya_copy(e, d).wait_recv()
-        zh = lax.rem(pair + part, 2)
-        swap = rcopy(wh.at[c, zh], wh.at[c, zh], s_c.at[1 + part], r_c.at[1 + part], core)
-        swap.start()
-        lax.fori_loop(2 * part, 2 * part + 2, project_own, 0)
-        swap.wait()
-        lax.fori_loop(2 * part, 2 * part + 2, project_rest, 0)
-    for e in range(1, 8):
-        za_copy(e).wait_send()
-        zb_copy(e).wait_send()
-        for d in (1, 2, 3):
-            ya_copy(e, d).wait_send()
+    def xforward(i, carry):
+        j = lax.rem(i + 2 * pair, CHUNKS)
+        for t in range(2):
+            xcopy(0, t, j).wait_recv()
+            mine_too = acc[j, lax.rem(x + 1 + 2 * t, NX), pl.ds(HR * t, HR)]
+            xro[t, j] = (mine_too + xrel[t, j].astype(F32)).astype(BF16)
+            xcopy(2, t, j).start()
+        return carry
+
+    lax.fori_loop(0, CHUNKS, project_own, 0)
+    for e in range(8):
+        swap(e).wait()
+    project_rest(0, 0)
+    xstart(0)
+    lax.fori_loop(1, CHUNKS, project_rest, 0)
+
+    def xstep(i, carry):
+        xsent(i - 1)
+        xstart(i)
+        xforward(i - 1, 0)
+        return carry
+
+    lax.fori_loop(1, CHUNKS, xstep, 0)
+    xsent(CHUNKS - 1)
+    xforward(CHUNKS - 1, 0)
+    for e in range(8):
+        if e > 0:
+            zcopy(e).wait_send()
+        for s in range(2):
+            ycopy(s, e).wait_send()
+            ypass(s, e).wait_send()
     load_hidden.wait()
 
     def layer_copy(j):
@@ -401,19 +486,19 @@
     def layer(i, carry):
         square, along = carry
         j = lax.rem(i + 2 * pair, CHUNKS)
-        for d in (1, 2, 3):
-            xcopy(d, j).wait()
+        for t in range(2):
+            xcopy(1, t, j).wait_recv()
+            xcopy(2, t, j).wait()
         cols = pl.ds(pl.multiple_of(j * CW, 128), CW)
         total = hv[:, cols].astype(F32) + acc[j, x]
-        for d in (1, 2, 3):
-            total += xr[d - 1, j].astype(F32)
+        for t in range(2):
+            total += xin[t, j].astype(F32)
         rounded = total.astype(BF16)
         lv[:, cols] = rounded
         layer_copy(j).start()
         value = rounded.astype(F32)
-        factor = gain[:, cols] * head[:, cols]
         square += jnp.sum(value * value, axis=1, keepdims=True)
-        along += jnp.sum(value * factor, axis=1, keepdims=True)
+        along += jnp.sum(value * factor[:, cols], axis=1, keepdims=True)
         return square, along
 
     zero = jnp.zeros((ROWS, 1), F32)
@@ -426,29 +511,51 @@
     partial = jnp.sum(inv * along * weight, axis=0, keepdims=True)
     rw[pair, x] = jnp.broadcast_to(partial, (8, 128))
     own_rw = rw.at[pair, x]
-    rw_copies = [rcopy(own_rw, own_rw, s_rw.at[i - 1], r_rw.at[i - 1], rwdev(i)) for i in range(1, 8)]
+    rw_far = rcopy(own_rw, own_rw, s_rw.at[0], r_rw.at[0], far)
+    rw_far.start()
+    both_rw = rw.at[:, x]
+    rw_copies = [rcopy(both_rw, both_rw, s_rw.at[d], r_rw.at[d], xdev(d)) for d in (1, 2, 3)]
+
+    gscale = inv * weight
+    gcorr = inv * inv * inv * along * weight * (1.0 / WIDTH)
+
+    def gcopy(kind, t, j):
+        if kind == 0:
+            part = gf.at[j, x]
+        else:
+            part = gf.at[j, lax.rem(x + 3 - 2 * t, NX), pl.ds(HR * t, HR)]
+        return rcopy(part, part, s_g.at[kind, t, j], r_g.at[kind, t, j], xdev(1 + 2 * t))
+
+    def rows_grad(i, carry):
+        j = lax.rem(i + 2 * pair, CHUNKS)
+        cols = pl.ds(pl.multiple_of(j * CW, 128), CW)
+        value = lv[:, cols].astype(F32)
+        gf[j, x] = (gscale * factor[:, cols] - value * gcorr).astype(BF16)
+        for t in range(2):
+            @pl.when(i < 1)
+            def _():
+                gcopy(0, t, j).start()
+        return carry
+
+    lax.fori_loop(0, CHUNKS, rows_grad, 0)
+
+    def gforward(i):
+        j = lax.rem(i + 2 * pair, CHUNKS)
+        for t in range(2):
+            gcopy(0, t, j).wait_send()
+        if i + 1 < CHUNKS:
+            for t in range(2):
+                gcopy(0, t, lax.rem(j + 1, CHUNKS)).start()
+        for t in range(2):
+            gcopy(0, t, j).wait_recv()
+        for t in range(2):
+            gcopy(1, t, j).start()
+
+    rw_far.wait()
     for cp in rw_copies:
         cp.start()
-
-    gscale = inv * weight
-    gcorr = inv * inv * inv * along * weight * (1.0 / WIDTH)
-
-    def gcopy(d, j):
-        own = gf.at[j, x]
-        return rcopy(own, own, s_g.at[d - 1, j], r_g.at[d - 1, j], xdev(d))
-
-    def rows_grad(i, carry):
-        j = lax.rem(i + 2 * pair, CHUNKS)
-        cols = pl.ds(pl.multiple_of(j * CW, 128), CW)
-        factor = gain[:, cols] * head[:, cols]
-        value = lv[:, cols].astype(F32)
-        gf[j, x] = (gscale * factor - value * gcorr).astype(BF16)
-        for d in (2, 1, 3):
-            gcopy(d, j).start()
-        return carry
-
-    lax.fori_loop(0, CHUNKS, rows_grad, 0)
-
+    gforward(0)
+    gforward(1)
     for cp in rw_copies:
         cp.wait()
     reward0 = rw[0, 0] + rw[0, 1] + rw[0, 2] + rw[0, 3]
@@ -467,8 +574,8 @@
 
     def products(i):
         j = lax.rem(i + 2 * pair, CHUNKS)
-        for d in (1, 2, 3):
-            gcopy(d, j).wait()
+        for t in range(2):
+            gcopy(1, t, j).wait()
         g = gf[j].reshape(TOK, CW)
         mo[j] = (mm(g, att[mate], TN) * slope).astype(BF16)
         mcopy(j).start()
@@ -476,11 +583,20 @@
         for half in range(2):
             gacc[half] += mm(g, wrows(half, j), NN)
 
-    def ycopy2(d, zh):
-        src = red.at[zh, lax.rem(y + d, NY), :, :, pl.ds(0, LA)]
-        return rcopy(src, yl.at[d - 1, zh], t_y.at[d - 1, zh], u_y.at[d - 1, zh], ydev(d))
-
-    def zcopy2(d, yp):
+    def ycopy2(kind, s, zh):
+        near = 1 + 2 * s
+        if kind == 0:
+            src = red.at[zh, lax.rem(y + 2, NY), pl.ds(2 * s, 2), :, pl.ds(0, LA)]
+            dst = yrel.at[s, zh]
+        elif kind == 1:
+            blocks = pl.ds(2 - 2 * s, 2)
+            src = red.at[zh, lax.rem(y + near, NY), blocks, :, pl.ds(0, LA)]
+            dst = yin.at[s, zh, blocks]
+        else:
+            src, dst = yro.at[s, zh], yin.at[s, zh, pl.ds(2 * s, 2)]
+        return rcopy(src, dst, t_y.at[kind, s, zh], u_y.at[kind, s, zh], ydev(near))
+
+    def zcopy3(d, yp):
         to = lax.rem(z + d, NZ)
         src = red.at[to // 4, pl.ds(2 * yp, 2), lax.rem(to, 4), :, pl.ds(LA, LB)]
         return rcopy(src, z2l.at[d - 1, yp], t_z2.at[d - 1, yp], u_z2.at[d - 1, yp], zdev(d))
@@ -492,23 +608,40 @@
         mcopy(j).wait()
         both = own[j] + mi[j].astype(F32)
         red[zh, pl.ds(yp * 2, 2)] = both.astype(BF16).reshape(2, 4, BLK, HALF)
-        for d in (2, 1, 3):
-            @pl.when(lax.rem(y + d, NY) // 2 == yp)
+
+        @pl.when(lax.rem(y + 2, NY) // 2 == yp)
+        def _():
+            for s in range(2):
+                ycopy2(0, s, zh).start()
+
+        for s in range(2):
+            @pl.when(lax.rem(y + 1 + 2 * s, NY) // 2 == yp)
             def _():
-                ycopy2(d, zh).start()
+                ycopy2(1, s, zh).start()
+
         for d in (4, 3, 5, 2, 6, 1, 7):
             @pl.when(lax.rem(z + d, NZ) // 4 == zh)
             def _():
-                zcopy2(d, yp).start()
-
-    def step(i, carry):
-        products(i)
-        merge(i - 1)
-        return carry
+                zcopy3(d, yp).start()
+
+    def yrelay(part):
+        zh = lax.rem(pair + part, 2)
+        for s in range(2):
+            ycopy2(0, s, zh).wait_recv()
+            mine_too = red[zh, lax.rem(y + 1 + 2 * s, NY), pl.ds(2 * s, 2), :, pl.ds(0, LA)].astype(F32)
+            yro[s, zh] = (mine_too + yrel[s, zh].astype(F32)).astype(BF16)
+            ycopy2(2, s, zh).start()
 
     products(0)
-    lax.fori_loop(1, CHUNKS, step, 0)
-    merge(CHUNKS - 1)
+    gforward(2)
+    products(1)
+    merge(0)
+    gforward(3)
+    products(2)
+    merge(1)
+    products(3)
+    merge(2)
+    merge(3)
 
     gatt[...] = gacc[...].astype(BF16)
     dk[...] = jnp.zeros_like(dk)
@@ -534,7 +667,7 @@
         dq_copy(h).start()
         return carry
 
-    def zcopy1(d):
+    def zcopy2(d):
         to = lax.rem(z + d, NZ)
         src = zsend.at[to // 4, lax.rem(to, 4)]
         return rcopy(src, zl.at[d - 1], t_z.at[d - 1], u_z.at[d - 1], zdev(d))
@@ -542,19 +675,20 @@
     def ysum(part):
         zh = lax.rem(pair + part, 2)
         total = red[zh, y, :, :, pl.ds(0, LA)].astype(F32)
-        for d in (1, 2, 3):
-            ycopy2(d, zh).wait_recv()
-            total += yl[d - 1, zh].astype(F32)
+        for s in range(2):
+            ycopy2(1, s, zh).wait_recv()
+            ycopy2(2, s, zh).wait_recv()
+            total += yin[s, zh].astype(F32)
         zsend[zh] = total.astype(BF16)
         for e in range(4 * part, 4 * part + 4):
             if e > 0:
-                zcopy1(hop(e)[1]).start()
+                zcopy2(hop(e)[1]).start()
 
     lax.fori_loop(0, 2, backward, 0)
-    ysum(0)
-    lax.fori_loop(2, 5, backward, 0)
-    ysum(1)
-    lax.fori_loop(5, HEADS, backward, 0)
+    yrelay(0)
+    lax.fori_loop(2, 6, backward, 0)
+    yrelay(1)
+    lax.fori_loop(6, HEADS, backward, 0)
 
     dkv_out[0] = (dk[TOK:, :] * slope_scaled).astype(BF16)
     dkv_out[1] = (dv[TOK:, :] * slope).astype(BF16)
@@ -562,32 +696,35 @@
     for cp in back:
         cp.start()
 
-    part = red[pair, :, zlo, :, pl.ds(LA, LB)].astype(F32).reshape(2, 2, BLK, LB)
+    ysum(0)
+    ysum(1)
+    total = red[pair, :, zlo, :, pl.ds(LA, LB)].astype(F32).reshape(2, 2, BLK, LB)
     for d in range(1, 8):
         for yp in range(2):
-            zcopy2(d, yp).wait()
-        part += z2l[d - 1].astype(F32)
-    y2send[...] = part.astype(BF16).reshape(NY, BLK, LB)
+            zcopy3(d, yp).wait()
+        total += z2l[d - 1].astype(F32)
+    y2send[...] = total.astype(BF16).reshape(NY, BLK, LB)
     yb2 = []
     for d in (2, 1, 3):
         src = y2send.at[lax.rem(y + d, NY)]
         yb2.append(rcopy(src, y2l.at[d - 1], t_y2.at[d - 1], u_y2.at[d - 1], ydev(d)))
         yb2[-1].start()
     for d in range(1, 8):
-        zcopy1(d).wait()
-    for d in (1, 2, 3):
-        for zh in range(2):
-            ycopy2(d, zh).wait_send()
-    part = zsend[pair, zlo].astype(F32)
+        zcopy2(d).wait()
+    for kind in range(3):
+        for s in range(2):
+            for zh in range(2):
+                ycopy2(kind, s, zh).wait_send()
+    total = zsend[pair, zlo].astype(F32)
     for d in range(7):
-        part += zl[d].astype(F32)
-    gwc[:, 0:LA] = part
+        total += zl[d].astype(F32)
+    gwc[:, 0:LA] = total
     for cp in yb2:
         cp.wait()
-    part = y2send[y].astype(F32)
+    total = y2send[y].astype(F32)
     for d in range(3):
-        part += y2l[d].astype(F32)
-    gwc[:, LA:] = part
+        total += y2l[d].astype(F32)
+    gwc[:, LA:] = total
     mate_rows = gwc.at[pl.ds(pl.multiple_of(mate * 40, 8), 40)]
     gswap = rcopy(mate_rows, gwr, s_c.at[3], r_c.at[3], core)
     gswap.start()
@@ -603,6 +740,12 @@
         cp.wait()
     dk_o[...] = (dk[0:TOK, :] * slope_scaled + dkv_in[0].astype(F32)).astype(BF16)
     dv_o[...] = (dv[0:TOK, :] * slope + dkv_in[1].astype(F32)).astype(BF16)
+
+
+def place(*refs):
+    for source, result in zip(refs[:5], refs[6:]):
+        result[...] = source[...]
+    refs[11][0] = jnp.max(refs[5][...])
 
 
 def per_device(hidden_in, queries, key_states, value_states, out_weight, norm_gain, reward_head, lengths, labels):
@@ -634,12 +777,21 @@
         key_states[0, 0],
         value_states[0, 0],
         out_weight.T,
-        norm_gain[None],
-        reward_head[None],
+        norm_gain,
+        reward_head,
     )
+    results = (layer_rows, grad_query, grad_keys, grad_values, grad_weight)
+    shapes = tuple(jax.ShapeDtypeStruct(r.shape, r.dtype) for r in results)
+    layer_rows, grad_query, grad_keys, grad_values, grad_weight, loss = pl.pallas_call(
+        place,
+        out_shape=shapes + (jax.ShapeDtypeStruct((1,), F32),),
+        in_specs=[vmem] * 6,
+        out_specs=(vmem,) * 5 + (smem,),
+        cost_estimate=pl.CostEstimate(flops=0, bytes_accessed=4 * 2**20, transcendentals=0),
+    )(*results, loss)
     return (
         layer_rows[None, None],
-        loss[0, 0:1],
+        loss,
         grad_query[None, None],
         grad_keys[None, None],
         grad_values[None, None],

time: 145 us -> 135 us (0.931)
  local copies, waits for them, and re-layouts: 7.95 us -> 0 us
    unnamed x15 -> x0, local copies, waits for them, and re-layouts: 4.76 us -> none
    pallas_call x1, Pallas kernels: 134 us -> 131 us  [per_device(): pl.pallas_call(kernel, out_shape=(jax.ShapeDtypeStruct((ROWS, WIDTH), BF1...]
    pallas_call x0 -> x1, Pallas kernels: none -> 2.56 us  [per_device(): pl.pallas_call(place, out_shape=shapes + (jax.ShapeDtypeStruct((1,), F32)...]
    broadcast_in_dim x2 -> x0, local copies, waits for them, and re-layouts: 1.92 us -> none  [the longest x1 1.32 us: per_device(): norm_gain[None]]
where the time goes in v2:
time: 135 us
  Pallas kernels  133 us (99%)
  between operations  1.47 us (1%)
    pallas_call x1, Pallas kernels, per_device(): pl.pallas_call(kernel, out_shape=(jax.ShapeDtypeStruct((ROWS, WIDTH), BF1...  131 us

profile of v2, /device:TPU:1, one launch (start us, length us, event | category | flops | bytes accessed | tf_op | source)
XLA Modules:
  0.0 134.7 jit_solution(5888914059169248092)
XLA Ops:
  1.3 130.7 %shard_map.136 = (bf16[96,2560]{1,0:T(8,128)(2,1)}, f32[8,128]{1,0:T(8,128)}, bf16[384,1024]{1,0:T(8,128)(2,1)}, bf16[384,128]{1,0:T(8,128)(2,1)}, bf16[384,128]{1,0:T(8,128)(2,1)}, /*index=5*/f32[40,1024]{1,0:T(8,128)}) custom-call(s32[1,2]{1,0:T(1,128)} %refs_0_.1, s32[1]{0:T(128)S(6)} %copy.15.refs_1_, bf16[96,2560]{1,0:T(8,128)(2,1)} %bitcast.12, ...), custom_call_target="tpu_custom_call" | custom-call | flops 12000000000 | bytes 10485760 | tf_op jit(solution)/shard_map/pallas_call | solution.py:755
  132.0 2.6 %shard_map.137 = (bf16[96,2560]{1,0:T(8,128)(2,1)}, bf16[384,1024]{1,0:T(8,128)(2,1)}, bf16[384,128]{1,0:T(8,128)(2,1)}, bf16[384,128]{1,0:T(8,128)(2,1)}, f32[40,1024]{1,0:T(8,128)}, /*index=5*/f32[1]{0:T(128)}) custom-call(bf16[96,2560]{1,0:T(8,128)(2,1)} %get-tuple-element.18.refs_0_, bf16[384,1024]{1,0:T(8,128)(2,1)} %get-tuple-element.19.refs_1_, ...), custom_call_target="tpu_custom_call" | custom-call | bytes 4194304 | tf_op jit(solution)/shard_map/pallas_call | solution.py:785

commit v3 on v2

--- a/solution.py
+++ b/solution.py
@@ -83,6 +83,8 @@
     peak=pltpu.VMEM((HEADS, 1, TOK), F32),
     mass=pltpu.VMEM((HEADS, 1, TOK), F32),
     part_out=pltpu.VMEM((HEADS, HEAD_DIM, TOK), F32),
+    probs=pltpu.VMEM((HEADS, 2 * TOK, TOK), BF16),
+    dscores=pltpu.VMEM((HEADS, 2 * TOK, TOK), BF16),
     lse=pltpu.VMEM((HEADS, 1, TOK), F32),
     att=pltpu.VMEM((2, TOK, HALF), BF16),
     acc=pltpu.VMEM((CHUNKS, NX, ROWS, CW), F32),
@@ -101,7 +103,10 @@
     yro=pltpu.VMEM((2, 2, 2, BLK, LA), BF16),
     zsend=pltpu.VMEM((2, 4, BLK, LA), BF16),
     zl=pltpu.VMEM((7, BLK, LA), BF16),
-    z2l=pltpu.VMEM((7, 2, 2, BLK, LB), BF16),
+    z2l=pltpu.VMEM((2, 2, 2, 2, BLK, LB), BF16),
+    z2third=pltpu.VMEM((2, 2, 2, BLK, LB), BF16),
+    z2fourth=pltpu.VMEM((2, 2, 1, BLK, LB), BF16),
+    z2out=pltpu.VMEM((2, 2, 2, BLK, LB), BF16),
     y2send=pltpu.VMEM((NY, BLK, LB), BF16),
     y2l=pltpu.VMEM((3, BLK, LB), BF16),
     factor=pltpu.VMEM((1, WIDTH), F32),
@@ -135,8 +140,8 @@
     u_z=DMA((7,)),
     t_y=DMA((3, 2, 2)),
     u_y=DMA((3, 2, 2)),
-    t_z2=DMA((7, 2)),
-    u_z2=DMA((7, 2)),
+    t_z2=DMA((4, 2, 2)),
+    u_z2=DMA((4, 2, 2)),
     loc=DMA((8,)),
     out_l=DMA((CHUNKS,)),
     out_q=DMA((HEADS,)),
@@ -181,6 +186,8 @@
     peak = n.peak
     mass = n.mass
     part_out = n.part_out
+    probs = n.probs
+    dscores = n.dscores
     lse = n.lse
     att = n.att
     acc = n.acc
@@ -200,6 +207,9 @@
     zsend = n.zsend
     zl = n.zl
     z2l = n.z2l
+    z2third = n.z2third
+    z2fourth = n.z2fourth
+    z2out = n.z2out
     y2send = n.y2send
     y2l = n.y2l
     factor = n.factor
@@ -403,10 +413,8 @@
     lax.fori_loop(0, 2, forward_far, 0)
     yforward(7)
     hand(5)
-    lax.fori_loop(2, 6, forward_far, 0)
+    lax.fori_loop(2, HEADS, forward_far, 0)
     hand(6)
-    hand(7)
-    lax.fori_loop(6, HEADS, forward_far, 0)
 
     def wrows(half, j):
         return wh[half, j // 2, pl.ds(lax.rem(j, 2) * 2, 2)].reshape(CW, HALF)
@@ -455,22 +463,34 @@
             xcopy(2, t, j).start()
         return carry
 
-    lax.fori_loop(0, CHUNKS, project_own, 0)
-    for e in range(8):
+    def probability(h, carry):
+        cols = pl.ds(pl.multiple_of(h * HEAD_DIM, HEAD_DIM), HEAD_DIM)
+        s = mm(kall[...], qv[:, cols], NT) * scale2 + bias[...]
+        probs[h] = jnp.exp2(s - lse[h]).astype(BF16)
+        return carry
+
+    lax.fori_loop(0, 2, project_own, 0)
+    for e in range(7):
         swap(e).wait()
     project_rest(0, 0)
     xstart(0)
-    lax.fori_loop(1, CHUNKS, project_rest, 0)
+    project_rest(1, 0)
+    hand(7)
+    lax.fori_loop(2, CHUNKS, project_own, 0)
+    swap(7).wait()
+    lax.fori_loop(2, CHUNKS, project_rest, 0)
 
     def xstep(i, carry):
         xsent(i - 1)
         xstart(i)
         xforward(i - 1, 0)
+        lax.fori_loop(2 * i - 2, 2 * i, probability, 0)
         return carry
 
     lax.fori_loop(1, CHUNKS, xstep, 0)
     xsent(CHUNKS - 1)
     xforward(CHUNKS - 1, 0)
+    lax.fori_loop(6, HEADS, probability, 0)
     for e in range(8):
         if e > 0:
             zcopy(e).wait_send()
@@ -527,7 +547,7 @@
         return rcopy(part, part, s_g.at[kind, t, j], r_g.at[kind, t, j], xdev(1 + 2 * t))
 
     def rows_grad(i, carry):
-        j = lax.rem(i + 2 * pair, CHUNKS)
+        j = i
         cols = pl.ds(pl.multiple_of(j * CW, 128), CW)
         value = lv[:, cols].astype(F32)
         gf[j, x] = (gscale * factor[:, cols] - value * gcorr).astype(BF16)
@@ -540,7 +560,7 @@
     lax.fori_loop(0, CHUNKS, rows_grad, 0)
 
     def gforward(i):
-        j = lax.rem(i + 2 * pair, CHUNKS)
+        j = i
         for t in range(2):
             gcopy(0, t, j).wait_send()
         if i + 1 < CHUNKS:
@@ -573,7 +593,7 @@
     gacc[...] = jnp.zeros_like(gacc)
 
     def products(i):
-        j = lax.rem(i + 2 * pair, CHUNKS)
+        j = i
         for t in range(2):
             gcopy(1, t, j).wait()
         g = gf[j].reshape(TOK, CW)
@@ -596,15 +616,40 @@
             src, dst = yro.at[s, zh], yin.at[s, zh, pl.ds(2 * s, 2)]
         return rcopy(src, dst, t_y.at[kind, s, zh], u_y.at[kind, s, zh], ydev(near))
 
-    def zcopy3(d, yp):
+    def zblock(d, yp):
         to = lax.rem(z + d, NZ)
-        src = red.at[to // 4, pl.ds(2 * yp, 2), lax.rem(to, 4), :, pl.ds(LA, LB)]
-        return rcopy(src, z2l.at[d - 1, yp], t_z2.at[d - 1, yp], u_z2.at[d - 1, yp], zdev(d))
+        return to // 4, pl.ds(2 * yp, 2), lax.rem(to, 4), slice(None), pl.ds(LA, LB)
+
+    def zcopy3(kind, s, yp):
+        near, over = (1, NZ - 1)[s], (2, NZ - 2)[s]
+        sems = t_z2.at[kind, s, yp], u_z2.at[kind, s, yp]
+        if kind == 0:
+            return rcopy(red.at[zblock(near, yp)], z2l.at[s, 0, yp], *sems, zdev(near))
+        if kind == 1:
+            return rcopy(red.at[zblock((3, 5)[s], yp)], z2third.at[s, yp], *sems, zdev(near))
+        if kind == 2:
+            to = lax.rem(z + 4, NZ)
+            src = red.at[to // 4, pl.ds(2 * yp + s, 1), lax.rem(to, 4), :, pl.ds(LA, LB)]
+            return rcopy(src, z2fourth.at[s, yp], *sems, zdev(over))
+        return rcopy(z2out.at[s, yp], z2l.at[s, 1, yp], *sems, zdev(over))
+
+    def zrelay(i):
+        zh, yp = i // 2, i % 2
+        for s in range(2):
+            over = (2, NZ - 2)[s]
+
+            @pl.when(lax.rem(z + over, NZ) // 4 == zh)
+            def _():
+                zcopy3(1, s, yp).wait_recv()
+                zcopy3(2, s, yp).wait_recv()
+                both = red[zblock(over, yp)].astype(F32) + z2third[s, yp].astype(F32)
+                z2out[s, yp, 1 - s] = both[1 - s].astype(BF16)
+                z2out[s, yp, s] = (both[s] + z2fourth[s, yp, 0].astype(F32)).astype(BF16)
+                zcopy3(3, s, yp).start()
 
     def merge(i):
-        j = lax.rem(i + 2 * pair, CHUNKS)
-        zh = j // 2
-        yp = lax.rem(j, 2)
+        j = i
+        zh, yp = j // 2, j % 2
         mcopy(j).wait()
         both = own[j] + mi[j].astype(F32)
         red[zh, pl.ds(yp * 2, 2)] = both.astype(BF16).reshape(2, 4, BLK, HALF)
@@ -619,13 +664,13 @@
             def _():
                 ycopy2(1, s, zh).start()
 
-        for d in (4, 3, 5, 2, 6, 1, 7):
-            @pl.when(lax.rem(z + d, NZ) // 4 == zh)
-            def _():
-                zcopy3(d, yp).start()
-
-    def yrelay(part):
-        zh = lax.rem(pair + part, 2)
+        for kind, spans in ((2, (4, 4)), (1, (3, 5)), (0, (1, 7))):
+            for s in range(2):
+                @pl.when(lax.rem(z + spans[s], NZ) // 4 == zh)
+                def _():
+                    zcopy3(kind, s, yp).start()
+
+    def yrelay(zh):
         for s in range(2):
             ycopy2(0, s, zh).wait_recv()
             mine_too = red[zh, lax.rem(y + 1 + 2 * s, NY), pl.ds(2 * s, 2), :, pl.ds(0, LA)].astype(F32)
@@ -639,8 +684,10 @@
     gforward(3)
     products(2)
     merge(1)
+    zrelay(0)
     products(3)
     merge(2)
+    zrelay(1)
     merge(3)
 
     gatt[...] = gacc[...].astype(BF16)
@@ -655,15 +702,19 @@
     def backward(h, carry):
         cols = pl.ds(pl.multiple_of(h * HEAD_DIM, HEAD_DIM), HEAD_DIM)
         lane = pl.ds(pl.multiple_of(lax.rem(h, 4) * HEAD_DIM, HEAD_DIM), HEAD_DIM)
-        qh = qv[:, cols]
         gh = gatt[h // 4, :, lane]
-        p = jnp.exp2(mm(kall[...], qh, NT) * scale2 + bias[...] - lse[h])
+        p = probs[h].astype(F32)
         dprob = mm(vall[...], gh, NT)
         delta = jnp.sum(p * dprob, axis=0, keepdims=True)
-        ds = (p * (dprob - delta)).astype(BF16)
-        dv[...] += mm(p.astype(BF16), gh, NN)
-        dk[...] += mm(ds, qh, NN)
-        dqv[:, cols] = (jnp.transpose(mm(ktr[...], ds, NN)) * slope_scaled).astype(BF16)
+        dscores[h] = (p * (dprob - delta)).astype(BF16)
+        dv[...] += mm(probs[h], gh, NN)
+        dk[TOK:, :] += mm(dscores[h, TOK:, :], qv[:, cols], NN)
+        return carry
+
+    def backward_rest(h, carry):
+        cols = pl.ds(pl.multiple_of(h * HEAD_DIM, HEAD_DIM), HEAD_DIM)
+        dk[0:TOK, :] += mm(dscores[h, 0:TOK, :], qv[:, cols], NN)
+        dqv[:, cols] = (jnp.transpose(mm(ktr[...], dscores[h], NN)) * slope_scaled).astype(BF16)
         dq_copy(h).start()
         return carry
 
@@ -672,23 +723,28 @@
         src = zsend.at[to // 4, lax.rem(to, 4)]
         return rcopy(src, zl.at[d - 1], t_z.at[d - 1], u_z.at[d - 1], zdev(d))
 
-    def ysum(part):
-        zh = lax.rem(pair + part, 2)
+    def ysum(zh):
         total = red[zh, y, :, :, pl.ds(0, LA)].astype(F32)
         for s in range(2):
             ycopy2(1, s, zh).wait_recv()
             ycopy2(2, s, zh).wait_recv()
             total += yin[s, zh].astype(F32)
         zsend[zh] = total.astype(BF16)
-        for e in range(4 * part, 4 * part + 4):
-            if e > 0:
-                zcopy2(hop(e)[1]).start()
-
-    lax.fori_loop(0, 2, backward, 0)
+
+        @pl.when(pair != zh)
+        def _():
+            zcopy2(4).start()
+
+        for e in (1, 2, 3):
+            there = zh * 4 + lax.rem(zlo + e, 4)
+            zcopy2(lax.rem(there - z + NZ, NZ)).start()
+
+    lax.fori_loop(0, 3, backward, 0)
+    zrelay(2)
     yrelay(0)
-    lax.fori_loop(2, 6, backward, 0)
-    yrelay(1)
-    lax.fori_loop(6, HEADS, backward, 0)
+    lax.fori_loop(3, 5, backward, 0)
+    zrelay(3)
+    lax.fori_loop(5, HEADS, backward, 0)
 
     dkv_out[0] = (dk[TOK:, :] * slope_scaled).astype(BF16)
     dkv_out[1] = (dv[TOK:, :] * slope).astype(BF16)
@@ -696,13 +752,19 @@
     for cp in back:
         cp.start()
 
+    yrelay(1)
     ysum(0)
+    lax.fori_loop(0, HEADS, backward_rest, 0)
     ysum(1)
     total = red[pair, :, zlo, :, pl.ds(LA, LB)].astype(F32).reshape(2, 2, BLK, LB)
-    for d in range(1, 8):
-        for yp in range(2):
-            zcopy3(d, yp).wait()
-        total += z2l[d - 1].astype(F32)
+    for s in range(2):
+        for kind in range(4):
+            for yp in range(2):
+                zcopy3(kind, s, yp).wait_send()
+                if kind % 3 == 0:
+                    zcopy3(kind, s, yp).wait_recv()
+        for kind in range(2):
+            total += z2l[s, kind].astype(F32)
     y2send[...] = total.astype(BF16).reshape(NY, BLK, LB)
     yb2 = []
     for d in (2, 1, 3):

time: 135 us -> 128 us (0.948)
  Pallas kernels: 133 us -> 126 us
    pallas_call x1, Pallas kernels: 131 us -> 123 us  [per_device(): pl.pallas_call(kernel, out_shape=(jax.ShapeDtypeStruct((ROWS, WIDTH), BF1...]
where the time goes in v3:
time: 128 us; the launch traced here: 127 us
  Pallas kernels  126 us (98%)
  between operations  1.45 us (1%)
    pallas_call x1, Pallas kernels, per_device(): pl.pallas_call(kernel, out_shape=(jax.ShapeDtypeStruct((ROWS, WIDTH), BF1...  123 us
    pallas_call x1, Pallas kernels, per_device(): pl.pallas_call(place, out_shape=shapes + (jax.ShapeDtypeStruct((1,), F32)...  2.56 us

profile of v3, /device:TPU:1, one launch (start us, length us, event | category | flops | bytes accessed | tf_op | source)
XLA Modules:
  0.0 127.4 jit_solution(12094841842771010703)
XLA Ops:
  1.3 123.4 %shard_map.136 = (bf16[96,2560]{1,0:T(8,128)(2,1)}, f32[8,128]{1,0:T(8,128)}, bf16[384,1024]{1,0:T(8,128)(2,1)}, bf16[384,128]{1,0:T(8,128)(2,1)}, bf16[384,128]{1,0:T(8,128)(2,1)}, /*index=5*/f32[40,1024]{1,0:T(8,128)}) custom-call(s32[1,2]{1,0:T(1,128)} %refs_0_.1, s32[1]{0:T(128)S(6)} %copy.15.refs_1_, bf16[96,2560]{1,0:T(8,128)(2,1)} %bitcast.12, ...), custom_call_target="tpu_custom_call" | custom-call | flops 12000000000 | bytes 10485760 | tf_op jit(solution)/shard_map/pallas_call | solution.py:817
  124.7 2.6 %shard_map.137 = (bf16[96,2560]{1,0:T(8,128)(2,1)}, bf16[384,1024]{1,0:T(8,128)(2,1)}, bf16[384,128]{1,0:T(8,128)(2,1)}, bf16[384,128]{1,0:T(8,128)(2,1)}, f32[40,1024]{1,0:T(8,128)}, /*index=5*/f32[1]{0:T(128)}) custom-call(bf16[96,2560]{1,0:T(8,128)(2,1)} %get-tuple-element.18.refs_0_, bf16[384,1024]{1,0:T(8,128)(2,1)} %get-tuple-element.19.refs_1_, ...), custom_call_target="tpu_custom_call" | custom-call | bytes 4194304 | tf_op jit(solution)/shard_map/pallas_call | solution.py:847

commit v4 on v3

--- a/solution.py
+++ b/solution.py
@@ -360,7 +360,7 @@
         for s in range(2):
             ycopy(s, e).start()
         yforward(e - 1)
-        if e == 3:
+        if e == 2:
             for cp in kv_copies:
                 cp.start()
         if e >= 3:
@@ -481,9 +481,9 @@
     lax.fori_loop(2, CHUNKS, project_rest, 0)
 
     def xstep(i, carry):
-        xsent(i - 1)
         xstart(i)
         xforward(i - 1, 0)
+        xsent(i - 1)
         lax.fori_loop(2 * i - 2, 2 * i, probability, 0)
         return carry
 

time: 128 us -> 128 us (level)
  no operation moved by 1% of the time
where the time goes in v4:
time: 128 us; the launch traced here: 127 us
  Pallas kernels  126 us (98%)
  between operations  1.45 us (1%)
    pallas_call x1, Pallas kernels, per_device(): pl.pallas_call(kernel, out_shape=(jax.ShapeDtypeStruct((ROWS, WIDTH), BF1...  123 us
    pallas_call x1, Pallas kernels, per_device(): pl.pallas_call(place, out_shape=shapes + (jax.ShapeDtypeStruct((1,), F32)...  2.56 us

profile of v4, /device:TPU:1, one launch (start us, length us, event | category | flops | bytes accessed | tf_op | source)
XLA Modules:
  0.0 127.3 jit_solution(15548624925188130711)
XLA Ops:
  1.3 123.3 %shard_map.136 = (bf16[96,2560]{1,0:T(8,128)(2,1)}, f32[8,128]{1,0:T(8,128)}, bf16[384,1024]{1,0:T(8,128)(2,1)}, bf16[384,128]{1,0:T(8,128)(2,1)}, bf16[384,128]{1,0:T(8,128)(2,1)}, /*index=5*/f32[40,1024]{1,0:T(8,128)}) custom-call(s32[1,2]{1,0:T(1,128)} %refs_0_.1, s32[1]{0:T(128)S(6)} %copy.15.refs_1_, bf16[96,2560]{1,0:T(8,128)(2,1)} %bitcast.12, ...), custom_call_target="tpu_custom_call" | custom-call | flops 12000000000 | bytes 10485760 | tf_op jit(solution)/shard_map/pallas_call | solution.py:817
  124.6 2.6 %shard_map.137 = (bf16[96,2560]{1,0:T(8,128)(2,1)}, bf16[384,1024]{1,0:T(8,128)(2,1)}, bf16[384,128]{1,0:T(8,128)(2,1)}, bf16[384,128]{1,0:T(8,128)(2,1)}, f32[40,1024]{1,0:T(8,128)}, /*index=5*/f32[1]{0:T(128)}) custom-call(bf16[96,2560]{1,0:T(8,128)(2,1)} %get-tuple-element.18.refs_0_, bf16[384,1024]{1,0:T(8,128)(2,1)} %get-tuple-element.19.refs_1_, ...), custom_call_target="tpu_custom_call" | custom-call | bytes 4194304 | tf_op jit(solution)/shard_map/pallas_call | solution.py:847
